TPU v7x, 256 devices: a whole 4x4x8 slice. The times are simulated.
256 devices in a mesh: head: 16 (over y_lo, x, core), seq: 16 (over z, y_hi).
Axes of the slice: x: 4, y: 4 (y_hi: 2, y_lo: 2; y = y_hi * 2 + y_lo), z: 8, core: 2. Of those that a mesh axis runs over, the one named last changes fastest.
Arguments:
- layer_input: bfloat16 [8192, 2048], P('seq'), may hold values from -6 to 6
- qkv_weight: bfloat16 [3, 2048, 2048], P(None, None, 'head'), may hold values from -0.1875 to 0.1875
- queries: bfloat16 [8192, 2048], P('seq', 'head'), may hold values from -6 to 6
- key_states: bfloat16 [8192, 2048], P('seq', 'head'), may hold values from -6 to 6
- value_states: bfloat16 [8192, 2048], P('seq', 'head'), may hold values from -6 to 6
- attn_out: bfloat16 [8192, 2048], P('seq', 'head'), may hold values from -4 to 4
- grad_out: bfloat16 [8192, 2048], P('seq', 'head'), may hold values from -24 to 24
- log_sum_exp: float32 [8192, 32], P('seq', 'head'), as said below
- frames: int32 [128], replicated, may hold values from 0 to 31, as said below
Outputs:
- input_grad: bfloat16 [8192, 2048], P('seq', 'head')
- weight_grad: float32 [3, 2048, 2048], P(None, 'seq', 'head')
Inputs may be any that keep to these rules, and one draw needn't show every extreme that they name: frames[0] is 0 and each next block has the same frame or the next one; there are exactly 32 frames of varying lengths. `log_sum_exp`: each entry lies within 0.75 of ln(n) + 0.5, where n is the number of keys visible to its token.
All inputs are finite; a program needn't handle non-finite values.
Results may differ from a plain program's by a relative error of at most 0.025.
Values may be sent and summed in bfloat16 or wider, within the bound.
A program may use at most 64 MiB of HBM per device.

v0:
```python
import jax
import jax.numpy as jnp
from jax import lax
from jax.sharding import PartitionSpec as P

BLOCK = 64


def attend(
    query_part, grad_part, stat_part, delta_part, key_part, value_part, visible, score_scale
):
    query_count = query_part.shape[0]
    key_count = key_part.shape[0]
    head_local = stat_part.shape[1]
    head_size = query_part.shape[1] // head_local
    query_heads = query_part.reshape(query_count, head_local, head_size)
    grad_heads = grad_part.reshape(query_count, head_local, head_size)
    key_heads = key_part.reshape(key_count, head_local, head_size)
    value_heads = value_part.reshape(key_count, head_local, head_size)
    scores = jnp.einsum("qhd,khd->hqk", query_heads, key_heads, preferred_element_type=jnp.float32)
    probs = jnp.where(visible[None], jnp.exp(scores * score_scale - stat_part.T[:, :, None]), 0.0)
    value_grad = jnp.einsum(
        "hqk,qhd->khd", probs.astype(jnp.bfloat16), grad_heads, preferred_element_type=jnp.float32
    )
    prob_grad = jnp.einsum(
        "qhd,khd->hqk", grad_heads, value_heads, preferred_element_type=jnp.float32
    )
    score_grad = (probs * (prob_grad - delta_part.T[:, :, None])).astype(jnp.bfloat16)
    query_grad = (
        jnp.einsum("hqk,khd->qhd", score_grad, key_heads, preferred_element_type=jnp.float32)
        * score_scale
    )
    key_grad = (
        jnp.einsum("hqk,qhd->khd", score_grad, query_heads, preferred_element_type=jnp.float32)
        * score_scale
    )
    return (
        query_grad.reshape(query_count, -1),
        key_grad.reshape(key_count, -1),
        value_grad.reshape(key_count, -1),
    )


def block_grads(operands, visible, score_scale):
    return attend(*operands, visible, score_scale)


def local(
    layer_input,
    qkv_weight,
    queries,
    key_states,
    value_states,
    attn_out,
    grad_out,
    log_sum_exp,
    frames,
):
    tok_local, cols_local = queries.shape
    head_local = log_sum_exp.shape[1]
    head_size = cols_local // head_local
    score_scale = head_size ** (-0.5)
    seq_count = lax.axis_size("seq")
    total_rows = tok_local * seq_count
    own_start = lax.axis_index("seq") * tok_local
    all_frames = jnp.repeat(frames, BLOCK, total_repeat_length=total_rows)
    own_frames = lax.dynamic_slice_in_dim(all_frames, own_start, tok_local, 0)
    row_delta = jnp.sum(
        (grad_out.astype(jnp.float32) * attn_out.astype(jnp.float32)).reshape(
            tok_local, head_local, head_size
        ),
        axis=2,
    )
    all_keys, all_values = (
        lax.all_gather(key_states, "seq", axis=0, tiled=True),
        lax.all_gather(value_states, "seq", axis=0, tiled=True),
    )
    block_rows = min(1024, total_rows)
    step_indices = jnp.arange(total_rows // block_rows, dtype=jnp.int32)

    def key_step(running, block_index):
        row_start = block_index * block_rows
        key_frames = lax.dynamic_slice_in_dim(all_frames, row_start, block_rows, 0)
        visible = key_frames[None, :] <= own_frames[:, None]
        operands = (
            queries,
            grad_out,
            log_sum_exp,
            row_delta,
            lax.dynamic_slice_in_dim(all_keys, row_start, block_rows, 0),
            lax.dynamic_slice_in_dim(all_values, row_start, block_rows, 0),
        )
        query_part, key_part, value_part = block_grads(operands, visible, score_scale)
        return (running + query_part, (key_part, value_part))

    query_sum, (key_terms, value_terms) = lax.scan(
        key_step, jnp.zeros((tok_local, cols_local), jnp.float32), step_indices
    )
    key_sum, value_sum = (
        lax.psum_scatter(
            key_terms.reshape(total_rows, cols_local).astype(jnp.bfloat16),
            "seq",
            scatter_dimension=0,
            tiled=True,
        ).astype(jnp.float32),
        lax.psum_scatter(
            value_terms.reshape(total_rows, cols_local).astype(jnp.bfloat16),
            "seq",
            scatter_dimension=0,
            tiled=True,
        ).astype(jnp.float32),
    )
    grads = jnp.stack([query_sum, key_sum, value_sum]).astype(jnp.bfloat16)
    weight_terms = jnp.einsum("td,mtc->mdc", layer_input, grads, preferred_element_type=jnp.float32)
    weight_grad = lax.psum_scatter(
        weight_terms.astype(jnp.bfloat16), "seq", scatter_dimension=1, tiled=True
    ).astype(jnp.float32)
    input_terms = jnp.einsum("mtc,mdc->td", grads, qkv_weight, preferred_element_type=jnp.float32)
    input_grad = lax.psum_scatter(
        input_terms.astype(jnp.bfloat16), "head", scatter_dimension=1, tiled=True
    )
    return (input_grad, weight_grad)


def solution(mesh):
    placed = (
        P("seq", None),
        P(None, None, "head"),
        P("seq", "head"),
        P("seq", "head"),
        P("seq", "head"),
        P("seq", "head"),
        P("seq", "head"),
        P("seq", "head"),
        P(),
    )
    return jax.shard_map(
        local,
        mesh=mesh,
        in_specs=placed,
        out_specs=(P("seq", "head"), P(None, "seq", "head")),
        check_vma=False,
    )
```

profile of v0, /device:TPU:2, one launch (start us, length us, event | category | flops | bytes accessed | tf_op | source)
XLA Modules:
  0.0 991.6 jit_solution(5183779030204767862)
XLA Ops:
  7.2 1.8 copy.40
  14.9 48.9 %gather_fusion = s32[8192]{0:T(1024)S(1)} fusion(s32[128]{0:T(128)S(1)} %copy-done.1, s32[8192]{0:T(1024)S(1)} %broadcast_clamp_fusion), kind=kCustom, calls=%fused_computation | custom fusion | bytes 98304 | tf_op jit(solution)/shard_map/jit(_take)/gather | solution.py:66
  64.0 35.0 %all-gather.3.cloned.1.call-done = bf16[8192,128]{0,1:T(8,128)(2,1)} async-done(((bf16[512,128]{0,1:T(8,128)(2,1)}), bf16[8192,128]{0,1:T(8,128)(2,1)}) %all-gather.3.cloned.1.call-update) | async-done | bytes 2097168 | tf_op jit(solution)/shard_map/all_gather | solution.py:75
  99.0 84.7 %all-gather.5.cloned.1.call-done = bf16[8192,128]{0,1:T(8,128)(2,1)} async-done(((bf16[512,128]{0,1:T(8,128)(2,1)}), bf16[8192,128]{0,1:T(8,128)(2,1)}) %all-gather.5.cloned.1.call-update) | async-done | bytes 2097168 | tf_op jit(solution)/shard_map/all_gather | solution.py:76
  183.6 104.9 %while.16 = (s32[]{:T(128)}, f32[512,128]{0,1:T(8,128)S(1)}, bf16[8,1024,128]{1,2,0:T(8,128)(2,1)}, bf16[8,1024,128]{1,2,0:T(8,128)(2,1)}, s32[8]{0:T(128)S(1)},...) while((s32[]{:T(128)}, f32[512,128]{0,1:T(8,128)S(1)}, ...), condition=%wide.region_2.3_spmd.clone, body=%wide.region_1.2_spmd.clone.sunk | while | flops 682557440 | bytes 59009356 | solution.py:96
  191.6 3.5 fusion.47
  204.8 3.5 fusion.47
  217.9 3.5 fusion.47
  231.0 3.5 fusion.47
  244.1 3.5 fusion.47
  257.2 3.5 fusion.47
  270.3 3.5 fusion.47
  283.4 3.5 fusion.47
  288.5 3.9 copy.48
  292.5 3.9 copy.47
  296.6 200.7 %reduce-scatter.11.cloned.1.call-done = bf16[512,128]{1,0:T(8,128)(2,1)} async-done(((bf16[8192,128]{1,0:T(8,128)(2,1)}), bf16[512,128]{1,0:T(8,128)(2,1)}) %reduce-scatter.11.cloned.1.call-update) | async-done | bytes 131088 | tf_op jit(solution)/shard_map/reduce_scatter | solution.py:106
  497.3 209.5 %reduce-scatter.9.cloned.1.call-done = bf16[512,128]{1,0:T(8,128)(2,1)} async-done(((bf16[8192,128]{1,0:T(8,128)(2,1)}), bf16[512,128]{1,0:T(8,128)(2,1)}) %reduce-scatter.9.cloned.1.call-update) | async-done | bytes 131088 | tf_op jit(solution)/shard_map/reduce_scatter | solution.py:100
  706.8 3.1 fusion.7
  709.9 4.2 copy.57
  714.1 3.1 copy.61
  717.3 4.0 bitcast_convert_fusion
  721.3 3.9 copy.55
  725.3 195.5 %reduce-scatter.15.cloned.1.call-done = bf16[128,384]{1,0:T(8,128)(2,1)} async-done(((bf16[2048,384]{1,0:T(8,128)(2,1)}), bf16[128,384]{1,0:T(8,128)(2,1)}) %reduce-scatter.15.cloned.1.call-update) | async-done | bytes 98320
  922.6 60.5 %reduce-scatter.13.cloned.1.call-done = bf16[128,512]{1,0:T(8,128)(2,1)} async-done(((bf16[2048,512]{1,0:T(8,128)(2,1)}), bf16[128,512]{1,0:T(8,128)(2,1)}) %reduce-scatter.13.cloned.1.call-update) | async-done | bytes 131088
  (180 shorter events, 80.6 us)
Async XLA Ops:
  7.2 699.6 %copy-start = (bf16[512,2048]{1,0:T(8,128)(2,1)S(1)}, bf16[512,2048]{1,0:T(8,128)(2,1)}, u32[]{:S(2)}) copy-start(bf16[512,2048]{1,0:T(8,128)(2,1)} %param.13) | copy-start | bytes 6291460
  7.2 7.7 copy-start.1
  7.2 91.8 %all-gather.3.cloned.1.call-start = ((), (), s32[]{:S(2)}) async-start(), calls=%async_computation.4 | async-start | bytes 2228224 | tf_op jit(solution)/shard_map/all_gather | solution.py:75
  9.1 174.6 %all-gather.5.cloned.1.call-start = ((), (), s32[]{:S(2)}) async-start(), calls=%async_computation.5 | async-start | bytes 2228224 | tf_op jit(solution)/shard_map/all_gather | solution.py:76
  10.8 486.5 %reduce-scatter.11.cloned.1.call-start = ((), (), s32[]{:S(2)}) async-start(), calls=%async_computation.7 | async-start | bytes 2228224 | tf_op jit(solution)/shard_map/reduce_scatter | solution.py:106
  14.9 48.9 %copy-start.7 = (s32[64,128]{1,0:T(8,128)S(1)}, s32[64,128]{1,0:T(8,128)}, u32[]{:S(2)}) copy-start(s32[64,128]{1,0:T(8,128)} %constant.112.clone.1) | copy-start | bytes 98308
  14.9 168.8 %copy-start.8 = (f32[512,2]{0,1:T(2,128)S(1)}, f32[512,2]{0,1:T(2,128)}, u32[]{:S(2)}) copy-start(f32[512,2]{0,1:T(2,128)} %param.20) | copy-start | bytes 12292
  191.6 3.5 copy-start.3
  204.8 3.5 copy-start.3
  212.9 3.1 copy-start.4
  217.9 3.5 copy-start.3
  226.0 3.1 copy-start.4
  231.0 3.5 copy-start.3
  244.1 3.5 copy-start.3
  252.2 3.1 copy-start.4
  257.2 3.5 copy-start.3
  270.3 3.5 copy-start.3
  278.4 3.1 copy-start.4
  283.4 3.5 copy-start.3
  292.5 414.3 %reduce-scatter.9.cloned.1.call-start = ((), (), s32[]{:S(2)}) async-start(), calls=%async_computation.6 | async-start | bytes 2228224 | tf_op jit(solution)/shard_map/reduce_scatter | solution.py:100
  296.5 624.3 %reduce-scatter.15.cloned.1.call-start = ((), (), s32[]{:S(2)}) async-start(), calls=%async_computation.9 | async-start | bytes 1671168
  714.1 3.2 copy-start.5
  714.1 3.2 copy-start.6
  717.2 265.9 %reduce-scatter.13.cloned.1.call-start = ((), (), s32[]{:S(2)}) async-start(), calls=%async_computation.8 | async-start | bytes 2228224
  (12 other events, 23.1 us)
Sparse Core Ops, SparseCore 0:
  11.1 87.8 all-gather.2
  102.0 81.6 all-gather.4
  292.6 204.6 reduce-scatter.10
  501.1 205.6 reduce-scatter.8
  717.3 203.4 reduce-scatter.14
  923.3 59.7 reduce-scatter.12
where the time goes:
time: 996 us; the launch traced here: 992 us
  waiting for transfers between devices  786 us (79%)
  local copies, waits for them, and re-layouts  118 us (12%)
  matrix products  63.1 us (6%)
  between operations  14.3 us (1%)
    unnamed x8, waiting for transfers between devices  256 us
    reduce_scatter x1, waiting for transfers between devices, local(): lax.psum_scatter(key_terms.reshape(total_rows, cols_local).astype(jnp.bfl...  209 us
    reduce_scatter x1, waiting for transfers between devices, local(): lax.psum_scatter(value_terms.reshape(total_rows, cols_local).astype(jnp.b...  201 us
    all_gather x1, waiting for transfers between devices, local(): lax.all_gather(value_states, 'seq', axis=0, tiled=True)  84.7 us
    gather x1, local copies, waits for them, and re-layouts, local(): all_frames = jnp.repeat(frames, BLOCK, total_repeat_length=total_rows)  48.9 us
    all_gather x1, waiting for transfers between devices, local(): lax.all_gather(key_states, 'seq', axis=0, tiled=True)  35 us
    dot_general x8, matrix products, attend(): jnp.einsum('hqk,qhd->khd', probs.astype(jnp.bfloat16), grad_heads, prefer...  28 us
    unnamed x24, local copies, waits for them, and re-layouts  21.2 us
  transfers between devices with their start and end apart: 6, of which 6 were waited for; matrix products, arithmetic and copies ran while one was open for 7% of the time, Pallas kernels for 0%

commit v1 on v0

v1 whole, which is shorter than its diff:
```python
import functools

import jax
import jax.numpy as jnp
from jax import lax
from jax.experimental import pallas as pl
from jax.experimental.pallas import tpu as pltpu
from jax.sharding import PartitionSpec as P

BLOCK = 64
HEAD_SIZE = 64
COLS = 2 * HEAD_SIZE
FRAMES = 32
CHUNK = 256
HIDDEN = -16384.0
LOG2E = 1.4426950408889634
MESH = pl.DeviceIdType.MESH
BF16 = jnp.bfloat16
F32 = jnp.float32


def dot(left, right):
    return jnp.dot(left, right, preferred_element_type=F32)


def dot_nt(left, right):
    return lax.dot_general(left, right, (((1,), (1,)), ((), ())), preferred_element_type=F32)


def greet(peers):
    barrier = pltpu.get_barrier_semaphore()
    for peer in peers:
        pl.semaphore_signal(barrier, inc=1, device_id=peer, device_id_type=MESH)
    pl.semaphore_wait(barrier, len(peers))


def remote(source, target, send_sem, recv_sem, peer):
    return pltpu.make_async_remote_copy(
        src_ref=source,
        dst_ref=target,
        send_sem=send_sem,
        recv_sem=recv_sem,
        device_id=peer,
        device_id_type=MESH,
    )


def attention_kernel(
    nz,
    frames_ref,
    stat_ref,
    query_ref,
    key_ref,
    value_ref,
    out_ref,
    grad_ref,
    grads_ref,
    flipped_ref,
    key_other,
    value_other,
    slots,
    trail_send,
    trail_recv,
    key_wide,
    value_wide,
    key_flip,
    fixed,
    paired,
    score_low,
    key_sum,
    value_sum,
    own_query,
    part_send,
    part_recv,
    slot_sems,
    trail_sems,
    pair_sems,
):
    rows = query_ref.shape[0]
    half = rows // 2
    blocks = rows // BLOCK
    seq = lax.axis_index("seq")
    count = 2 * nz
    side = lax.rem(seq, 2)
    partner = seq + 1 - 2 * side
    up = lax.rem(seq + 2, count)
    down = lax.rem(seq + count - 2, count)
    ahead = ({"seq": up}, {"seq": down})
    greet(({"seq": partner}, {"seq": up}, {"seq": down}))

    pair_copies = [
        remote(key_ref, key_other, pair_sems.at[0, 0], pair_sems.at[1, 0], {"seq": partner}),
        remote(value_ref, value_other, pair_sems.at[0, 1], pair_sems.at[1, 1], {"seq": partner}),
    ]
    for copy in pair_copies:
        copy.start()

    def slot_copy(r, t):
        return remote(
            slots.at[r, t],
            slots.at[r, t + 1],
            slot_sems.at[0, r, t],
            slot_sems.at[1, r, t + 1],
            ahead[r],
        )

    def trail_copy(r, t):
        return remote(
            trail_send.at[r, t],
            trail_recv.at[r, t + 1],
            trail_sems.at[0, r, t],
            trail_sems.at[1, r, t + 1],
            ahead[r],
        )

    grad_wide = grad_ref[...].astype(F32)
    query_flip = jnp.transpose(query_ref[...].astype(F32) * (HEAD_SIZE**-0.5))
    grad_flip = jnp.transpose(grad_wide)
    delta_flip = jnp.transpose(grad_wide * out_ref[...].astype(F32))
    aux_row = lax.broadcasted_iota(jnp.int32, (16, rows), 0)
    aux = jnp.zeros((16, rows), F32)
    for h in range(2):
        delta = jnp.sum(
            delta_flip[h * HEAD_SIZE : (h + 1) * HEAD_SIZE, :], axis=0, keepdims=True
        )
        for first, value in ((3 * h, stat_ref[h : h + 1, :]), (6 + 3 * h, delta)):
            rest = value
            for place in range(3):
                piece = rest.astype(BF16).astype(F32)
                aux = jnp.where(aux_row == first + place, piece, aux)
                rest = rest - piece
    for r in range(2):
        lanes = slice(r * half, (r + 1) * half)
        slots[r, 0, 0:COLS, :] = query_flip[:, lanes].astype(BF16)
        slots[r, 0, COLS : 2 * COLS, :] = grad_flip[:, lanes].astype(BF16)
        slots[r, 0, 2 * COLS : 2 * COLS + 16, :] = aux[:, lanes].astype(BF16)
        slot_copy(r, 0).start()

    lane = lax.broadcasted_iota(jnp.int32, (BLOCK, COLS), 1)
    inner = lax.rem(lane, HEAD_SIZE)

    def build_keys(keys_from, values_from, base, owner):
        for b in range(blocks):
            here = slice(b * BLOCK, (b + 1) * BLOCK)
            there = slice(base + b * BLOCK, base + (b + 1) * BLOCK)
            frame = frames_ref[owner * blocks + b]
            keys = keys_from[here, :].astype(F32)
            values = values_from[here, :].astype(F32)
            for h in range(2):
                mine = (lane >= h * HEAD_SIZE) & (lane < (h + 1) * HEAD_SIZE)
                stat_at = (inner >= FRAMES + 3 * h) & (inner < FRAMES + 3 * h + 3)
                delta_at = (inner >= FRAMES + 6 + 3 * h) & (inner < FRAMES + 9 + 3 * h)
                key_more = jnp.where(inner == frame, 1.0, jnp.where(stat_at, -1.0, 0.0))
                value_more = jnp.where(delta_at, -1.0, 0.0)
                key_wide[h, there, :] = jnp.where(mine, keys, key_more).astype(BF16)
                value_wide[h, there, :] = jnp.where(mine, values, value_more).astype(BF16)
        key_flip[:, base : base + rows] = jnp.transpose(
            keys_from[...].astype(F32) * (HEAD_SIZE**-0.5)
        ).astype(BF16)

    frame_row = lax.broadcasted_iota(jnp.int32, (FRAMES, half), 0)
    frame_lane = lax.broadcasted_iota(jnp.int32, (FRAMES, half), 1)

    def prepare(r, t, owner):
        first = owner * blocks + r * (blocks // 2)
        seen = jnp.full((FRAMES, half), frames_ref[first + blocks // 2 - 1], jnp.int32)
        for i in range(blocks // 2 - 2, -1, -1):
            seen = jnp.where(frame_lane < (i + 1) * BLOCK, frames_ref[first + i], seen)
        hidden = jnp.where(frame_row > seen, HIDDEN, 0.0).astype(BF16)
        extra = jnp.concatenate(
            [hidden, slots[r, t, 2 * COLS : 2 * COLS + 16, :], jnp.zeros((16, half), BF16)], axis=0
        )
        zero = jnp.zeros((HEAD_SIZE, half), BF16)
        for which in range(2):
            low = slots[r, t, which * COLS : which * COLS + HEAD_SIZE, :]
            high = slots[r, t, which * COLS + HEAD_SIZE : (which + 1) * COLS, :]
            fixed[r, 2 * which, :, :] = jnp.concatenate([low, extra], axis=0)
            fixed[r, 2 * which + 1, :, :] = jnp.concatenate([extra, high], axis=0)
            paired[r, which, :, :] = jnp.concatenate(
                [jnp.concatenate([low, zero], axis=1), jnp.concatenate([zero, high], axis=1)], axis=0
            )

    def tile(r, start):
        here = pl.ds(start, CHUNK)
        probs, scores = [], []
        for h in range(2):
            score = dot(key_wide[h, here, :], fixed[r, h, :, :])
            prob = jnp.exp2(score * LOG2E)
            prob_grad = dot(value_wide[h, here, :], fixed[r, 2 + h, :, :])
            score_grad = (prob * prob_grad).astype(BF16)
            score_low[r, h, here, :] = score_grad
            probs.append(prob.astype(BF16))
            scores.append(score_grad)
        value_sum[here, :] += dot_nt(jnp.concatenate(probs, axis=1), paired[r, 1, :, :])
        key_sum[here, :] += dot_nt(jnp.concatenate(scores, axis=1), paired[r, 0, :, :])

    def tiles(first):
        for c in range(rows // CHUNK):
            for r in range(2):
                tile(r, pl.multiple_of(first + c * CHUNK, CHUNK))

    def query_part(r):
        return jnp.concatenate(
            [
                dot(key_flip[h * HEAD_SIZE : (h + 1) * HEAD_SIZE, :], score_low[r, h, :, :])
                for h in range(2)
            ],
            axis=0,
        )

    key_sum[...] = jnp.zeros_like(key_sum)
    value_sum[...] = jnp.zeros_like(value_sum)
    for r in range(2):
        trail_recv[r, 1, :, :] = jnp.zeros((COLS, half), BF16)
        prepare(r, 0, seq)
    build_keys(key_ref, value_ref, 0, seq)
    tiles(0)
    for copy in pair_copies:
        copy.wait()
    build_keys(key_other, value_other, rows, partner)
    tiles(rows)
    for r in range(2):
        own_query[:, r * half : (r + 1) * half] = query_part(r)

    def step(t, carry):
        for r in range(2):
            slot_copy(r, t - 1).wait_recv()

        @pl.when(t < nz - 1)
        def _():
            for r in range(2):
                slot_copy(r, t).start()

        prepare(0, t, lax.rem(seq + 2 * (nz - t), count))
        prepare(1, t, lax.rem(seq + 2 * t, count))

        def part(i, inner_carry):
            tiles(i * rows)
            return inner_carry

        lax.fori_loop(0, 2, part, 0)

        @pl.when(t > 1)
        def _():
            for r in range(2):
                trail_copy(r, t - 1).wait_recv()

        for r in range(2):
            total = query_part(r) + trail_recv[r, t, :, :].astype(F32)
            trail_send[r, t, :, :] = total.astype(BF16)
            trail_copy(r, t).start()
        return carry

    lax.fori_loop(1, nz, step, 0)

    part_send[0, :, :] = key_sum[rows:, :].astype(BF16)
    part_send[1, :, :] = value_sum[rows:, :].astype(BF16)
    part_copy = remote(part_send, part_recv, pair_sems.at[0, 2], pair_sems.at[1, 2], {"seq": partner})
    part_copy.start()

    for r in range(2):
        trail_copy(r, nz - 1).wait_recv()
        lanes = slice(r * half, (r + 1) * half)
        own_query[:, lanes] += trail_recv[r, nz, :, :].astype(F32)
    query_low = own_query[...].astype(BF16)
    flipped_ref[0:COLS, :] = query_low
    grads_ref[:, 0:COLS] = jnp.transpose(query_low.astype(F32)).astype(BF16)
    part_copy.wait_recv()
    for m, total in ((1, key_sum), (2, value_sum)):
        low = (total[0:rows, :] + part_recv[m - 1, :, :].astype(F32)).astype(BF16)
        grads_ref[:, m * COLS : (m + 1) * COLS] = low
        flipped_ref[m * COLS : (m + 1) * COLS, :] = jnp.transpose(low.astype(F32)).astype(BF16)

    part_copy.wait_send()
    for r in range(2):

        def drain(t, carry, r=r):
            slot_copy(r, t).wait_send()
            trail_copy(r, t + 1).wait_send()
            return carry

        lax.fori_loop(0, nz - 1, drain, 0)


def projection_kernel(
    nz,
    nx,
    input_ref,
    weight_ref,
    grads_ref,
    flipped_ref,
    input_out,
    weight_out,
    core_send,
    core_recv,
    x_send,
    x_recv,
    y_send,
    y_recv,
    z_send,
    z_recv,
    yh_send,
    yh_recv,
    core_sems,
    x_sems,
    y_sems,
    z_sems,
    yh_sems,
):
    seq = lax.axis_index("seq")
    head = lax.axis_index("head")
    count = 2 * nz
    side = lax.rem(seq, 2)
    z = seq // 2
    partner = {"seq": seq + 1 - 2 * side}
    z_ahead = ({"seq": lax.rem(seq + 2, count)}, {"seq": lax.rem(seq + count - 2, count)})
    core = lax.rem(head, 2)
    x = lax.rem(head // 2, nx)
    low_side = head // (2 * nx)
    twin = {"head": head + 1 - 2 * core}
    plane = low_side * 2 * nx + core
    x_ahead = (
        {"head": plane + 2 * lax.rem(x + 1, nx)},
        {"head": plane + 2 * lax.rem(x + nx - 1, nx)},
    )
    neighbour = {"head": (1 - low_side) * 2 * nx + 2 * x + core}
    greet((partner, *z_ahead, twin, *x_ahead, neighbour))

    def input_term(x_at, y_at, core_at):
        first = pl.multiple_of(((y_at * nx + x_at) * 2 + core_at) * COLS, COLS)
        weights = jnp.concatenate(
            [weight_ref[m, pl.ds(first, COLS), :] for m in range(3)], axis=1
        )
        return dot_nt(grads_ref[...], weights)

    def weight_term(z_at, side_at):
        first = pl.multiple_of((z_at * 2 + side_at) * COLS, COLS)
        return dot(flipped_ref[...], input_ref[:, pl.ds(first, COLS)])

    def reach(length, i):
        return (length - i) // 2

    def at(r, distance, position, length):
        return lax.rem(position + distance if r == 0 else position + length - distance, length)

    def half_of(r, i):
        return (i + r) % 2

    core_order = [(r, i) for i in range(nx - 1) for r in range(2)] + [(0, nx - 1), (0, nx)]
    core_copies = {}
    for place, (r, i) in enumerate(core_order):
        x_at = at(r, reach(nx, i), x, nx)
        y_at = half_of(r, i)
        core_send[place, :, :] = input_term(x_at, y_at, 1 - core).astype(BF16)
        copy = remote(
            core_send.at[place],
            core_recv.at[place],
            core_sems.at[0, place],
            core_sems.at[1, place],
            twin,
        )
        copy.start()
        core_copies[r, i] = (place, copy)

    started = [copy for _, copy in core_copies.values()]

    z_copies = {}

    def z_message(i):
        for r in range(2):
            total = weight_term(at(r, reach(nz, i), z, nz), half_of(r, i))
            if i >= 2:
                z_copies[r, i - 2].wait_recv()
                total = total + z_recv[r, i - 2, :, :].astype(F32)
            z_send[r, i, :, :] = total.astype(BF16)
            copy = remote(
                z_send.at[r, i], z_recv.at[r, i], z_sems.at[0, r, i], z_sems.at[1, r, i], z_ahead[r]
            )
            copy.start()
            z_copies[r, i] = copy
            started.append(copy)

    x_copies = {}

    def input_pair(r, i):
        place, copy = core_copies[r, i]
        total = input_term(at(r, reach(nx, i), x, nx), half_of(r, i), core)
        copy.wait_recv()
        return total + core_recv[place, :, :].astype(F32)

    def x_message(i):
        for r in range(2):
            total = input_pair(r, i)
            if i >= 2:
                x_copies[r, i - 2].wait_recv()
                total = total + x_recv[r, i - 2, :, :].astype(F32)
            x_send[r, i, :, :] = total.astype(BF16)
            copy = remote(
                x_send.at[r, i], x_recv.at[r, i], x_sems.at[0, r, i], x_sems.at[1, r, i], x_ahead[r]
            )
            copy.start()
            x_copies[r, i] = copy
            started.append(copy)

    def x_final(place):
        total = input_pair(0, nx - 1 + place)
        y_at = half_of(0, nx - 1 + place)
        for r in range(2):
            i = nx - 2 if half_of(r, nx - 2) == y_at else nx - 3
            x_copies[r, i].wait_recv()
            total = total + x_recv[r, i, :, :].astype(F32)
        return y_at, total

    def z_final(side_at):
        total = weight_term(z, side_at)
        for r in range(2):
            i = nz - 2 if half_of(r, nz - 2) == side_at else nz - 3
            z_copies[r, i].wait_recv()
            total = total + z_recv[r, i, :, :].astype(F32)
        return total

    z_message(0)
    z_message(1)
    x_message(0)
    x_message(1)
    z_message(2)
    x_message(2)
    z_message(3)
    finals = dict(x_final(place) for place in range(2))
    mine = jnp.where(low_side == 0, finals[0], finals[1])
    y_send[...] = jnp.where(low_side == 0, finals[1], finals[0]).astype(BF16)
    y_copy = remote(y_send, y_recv, y_sems.at[0], y_sems.at[1], neighbour)
    y_copy.start()
    for i in range(4, nz - 1):
        z_message(i)
    y_copy.wait_recv()
    input_out[...] = (mine + y_recv[...].astype(F32)).astype(BF16)
    sides = [z_final(side_at) for side_at in range(2)]
    kept = jnp.where(side == 0, sides[0], sides[1])
    yh_send[...] = jnp.where(side == 0, sides[1], sides[0]).astype(BF16)
    yh_copy = remote(yh_send, yh_recv, yh_sems.at[0], yh_sems.at[1], partner)
    yh_copy.start()
    yh_copy.wait_recv()
    total = kept + yh_recv[...].astype(F32)
    for m in range(3):
        weight_out[m, :, :] = jnp.transpose(total[m * COLS : (m + 1) * COLS, :])
    y_copy.wait_send()
    yh_copy.wait_send()
    for copy in started:
        copy.wait_send()


def local(
    nz,
    nx,
    layer_input,
    qkv_weight,
    queries,
    key_states,
    value_states,
    attn_out,
    grad_out,
    log_sum_exp,
    frames,
):
    rows = queries.shape[0]
    half = rows // 2
    vmem = pl.BlockSpec(memory_space=pltpu.VMEM)
    smem = pl.BlockSpec(memory_space=pltpu.SMEM)
    dma = pltpu.SemaphoreType.DMA
    grads, flipped = pl.pallas_call(
        functools.partial(attention_kernel, nz),
        out_shape=(
            jax.ShapeDtypeStruct((rows, 3 * COLS), BF16),
            jax.ShapeDtypeStruct((3 * COLS, rows), BF16),
        ),
        in_specs=[smem] + [vmem] * 6,
        out_specs=(vmem, vmem),
        scratch_shapes=[
            pltpu.VMEM((rows, COLS), BF16),
            pltpu.VMEM((rows, COLS), BF16),
            pltpu.VMEM((2, nz, 2 * COLS + 16, half), BF16),
            pltpu.VMEM((2, nz, COLS, half), BF16),
            pltpu.VMEM((2, nz + 1, COLS, half), BF16),
            pltpu.VMEM((2, 2 * rows, COLS), BF16),
            pltpu.VMEM((2, 2 * rows, COLS), BF16),
            pltpu.VMEM((COLS, 2 * rows), BF16),
            pltpu.VMEM((2, 4, COLS, half), BF16),
            pltpu.VMEM((2, 2, COLS, 2 * half), BF16),
            pltpu.VMEM((2, 2, 2 * rows, half), BF16),
            pltpu.VMEM((2 * rows, COLS), F32),
            pltpu.VMEM((2 * rows, COLS), F32),
            pltpu.VMEM((COLS, rows), F32),
            pltpu.VMEM((2, rows, COLS), BF16),
            pltpu.VMEM((2, rows, COLS), BF16),
            dma((2, 2, nz)),
            dma((2, 2, nz + 1)),
            dma((2, 3)),
        ],
        compiler_params=pltpu.CompilerParams(
            collective_id=0, has_side_effects=True, vmem_limit_bytes=48 * 2**20
        ),
        name="attention_ring",
    )(frames, log_sum_exp.T, queries, key_states, value_states, attn_out, grad_out)
    wide = 3 * COLS
    input_grad, weight_grad = pl.pallas_call(
        functools.partial(projection_kernel, nz, nx),
        out_shape=(
            jax.ShapeDtypeStruct((rows, COLS), BF16),
            jax.ShapeDtypeStruct((3, COLS, COLS), F32),
        ),
        in_specs=[vmem] * 4,
        out_specs=(vmem, vmem),
        scratch_shapes=[
            pltpu.VMEM((2 * nx, rows, COLS), BF16),
            pltpu.VMEM((2 * nx, rows, COLS), BF16),
            pltpu.VMEM((2, nx - 1, rows, COLS), BF16),
            pltpu.VMEM((2, nx - 1, rows, COLS), BF16),
            pltpu.VMEM((rows, COLS), BF16),
            pltpu.VMEM((rows, COLS), BF16),
            pltpu.VMEM((2, nz - 1, wide, COLS), BF16),
            pltpu.VMEM((2, nz - 1, wide, COLS), BF16),
            pltpu.VMEM((wide, COLS), BF16),
            pltpu.VMEM((wide, COLS), BF16),
            dma((2, 2 * nx)),
            dma((2, 2, nx - 1)),
            dma((2,)),
            dma((2, 2, nz - 1)),
            dma((2,)),
        ],
        compiler_params=pltpu.CompilerParams(
            collective_id=1, has_side_effects=True, vmem_limit_bytes=48 * 2**20
        ),
        name="projection_sums",
    )(layer_input, qkv_weight, grads, flipped)
    return input_grad, weight_grad


def solution(mesh):
    nz = mesh.shape["seq"] // 2
    nx = mesh.shape["head"] // 4
    placed = (
        P("seq", None),
        P(None, None, "head"),
        P("seq", "head"),
        P("seq", "head"),
        P("seq", "head"),
        P("seq", "head"),
        P("seq", "head"),
        P("seq", "head"),
        P(),
    )
    return jax.shard_map(
        functools.partial(local, nz, nx),
        mesh=mesh,
        in_specs=placed,
        out_specs=(P("seq", "head"), P(None, "seq", "head")),
        check_vma=False,
    )
```

time: 996 us -> 102 us (0.10)
  waiting for transfers between devices: 786 us -> 0 us
  local copies, waits for them, and re-layouts: 118 us -> 10.2 us
  Pallas kernels: 0 us -> 90.6 us
  matrix products: 63.1 us -> 0 us
  between operations: 14.3 us -> 0.67 us
    reduce_scatter x2 -> x0, waiting for transfers between devices: 410 us -> none  [the longest x1 209 us: local(): lax.psum_scatter(key_terms.reshape(total_rows, cols_local).astype(jnp.bfl...]
    unnamed x8 -> x0, waiting for transfers between devices: 256 us -> none
    all_gather x2 -> x0, waiting for transfers between devices: 120 us -> none  [the longest x1 84.7 us: local(): lax.all_gather(value_states, 'seq', axis=0, tiled=True)]
    pallas_call x0 -> x2, Pallas kernels: none -> 90.6 us  [the longest x1 59.8 us: local(): pl.pallas_call(functools.partial(attention_kernel, nz), out_shape=(jax.Sh...]
    dot_general x42 -> x0, matrix products: 63.1 us -> none  [the longest x8 28 us: attend(): jnp.einsum('hqk,qhd->khd', probs.astype(jnp.bfloat16), grad_heads, prefer...]
    gather x1 -> x0, local copies, waits for them, and re-layouts: 48.9 us -> none  [local(): all_frames = jnp.repeat(frames, BLOCK, total_repeat_length=total_rows)]
    dynamic_slice x33 -> x0, local copies, waits for them, and re-layouts: 21.9 us -> none  [the longest x8 9.32 us: key_step(): lax.dynamic_slice_in_dim(all_values, row_start, block_rows, 0)]
    unnamed x24 -> x20, local copies, waits for them, and re-layouts: 21.2 us -> 10.2 us
  transfers between devices with their start and end apart: 6 -> 0, of which waited for: 6 -> 0; matrix products, arithmetic and copies ran while one was open for 7% -> 0% of each run, Pallas kernels for 0% -> 0%
where the time goes in v1:
time: 102 us; the launch traced here: 101 us
  Pallas kernels  90.6 us (89%)
  local copies, waits for them, and re-layouts  10.2 us (10%)
    pallas_call x1, Pallas kernels, local(): pl.pallas_call(functools.partial(attention_kernel, nz), out_shape=(jax.Sh...  59.8 us
    pallas_call x1, Pallas kernels, local(): pl.pallas_call(functools.partial(projection_kernel, nz, nx), out_shape=(j...  30.8 us
    unnamed x20, local copies, waits for them, and re-layouts  10.2 us

profile of v1, /device:TPU:2, one launch (start us, length us, event | category | flops | bytes accessed | tf_op | source)
XLA Modules:
  0.0 101.5 jit_solution(7934618871670662173)
XLA Ops:
  0.6 0.0 copy-start.2
  0.6 0.9 copy-done.2
  1.5 0.0 copy-start.3
  1.5 0.9 copy-done.3
  2.4 0.0 copy-start.4
  2.4 0.9 copy-done.4
  3.3 0.0 copy-start.5
  3.3 0.9 copy-done.5
  4.3 0.0 copy-start.6
  4.3 0.9 copy-done.6
  5.2 0.0 copy-start.7
  5.2 0.7 copy-done.7
  5.8 0.0 copy-start.8
  5.8 0.7 copy-done.8
  6.5 59.8 %attention_ring.1 = (bf16[512,384]{1,0:T(8,128)(2,1)S(1)}, bf16[384,512]{1,0:T(8,128)(2,1)S(1)}) custom-call(s32[128]{0:T(128)S(1)} %copy-done.8, f32[2,512]{1,0:T(2,128)S(1)} %bitcast.1, bf16[512,128]{1,0:T(8,128)(2,1)S(1)} %copy-done.2, bf16[512,128]{1,0:T(8,128)(2,1)S(1)} %copy-done.3, bf16[512,128]{1,0:T(8,128)(2,1)S(1)} %copy-done.4, ...), custom_call_target="tpu_custom_call" | custom-call | tf_op jit(solution)/shard_map/attention_ring/pallas_call | solution.py:471
  66.3 0.0 copy-start
  66.3 1.6 %copy-done = bf16[512,2048]{1,0:T(8,128)(2,1)S(1)} copy-done((bf16[512,2048]{1,0:T(8,128)(2,1)S(1)}, bf16[512,2048]{1,0:T(8,128)(2,1)}, u32[]{:S(2)}) %copy-start) | copy-done | bytes 2097176
  67.9 0.0 copy-start.1
  67.9 1.4 %copy-done.1 = bf16[3,2048,128]{2,1,0:T(8,128)(2,1)S(1)} copy-done((bf16[3,2048,128]{2,1,0:T(8,128)(2,1)S(1)}, bf16[3,2048,128]{2,1,0:T(8,128)(2,1)}, u32[]{:S(2)}) %copy-start.1) | copy-done | bytes 1572888
  69.3 30.8 %projection_sums.1 = (bf16[512,128]{1,0:T(8,128)(2,1)S(1)}, f32[3,128,128]{2,1,0:T(8,128)S(1)}) custom-call(bf16[512,2048]{1,0:T(8,128)(2,1)S(1)} %copy-done, bf16[3,2048,128]{2,1,0:T(8,128)(2,1)S(1)} %copy-done.1, bf16[512,384]{1,0:T(8,128)(2,1)S(1)} %get-tuple-element.4.grads_ref, bf16[384,512]{1,0:T(8,128)(2,1)S(1)} %get-tuple-element.5.flipped_ref), custom_call_target="tpu_custom_call" | custom-call | tf_op jit(solution)/shard_map/projection_sums/pallas_call | solution.py:506
  100.1 0.7 copy.13
  100.8 0.7 copy.14
Async XLA Ops:
  0.6 0.9 copy-start.2
  1.5 0.9 copy-start.3
  2.4 0.9 copy-start.4
  3.3 0.9 copy-start.5
  4.3 0.9 copy-start.6
  5.2 0.7 copy-start.7
  5.8 0.7 copy-start.8
  66.3 1.6 %copy-start = (bf16[512,2048]{1,0:T(8,128)(2,1)S(1)}, bf16[512,2048]{1,0:T(8,128)(2,1)}, u32[]{:S(2)}) copy-start(bf16[512,2048]{1,0:T(8,128)(2,1)} %input_ref.1) | copy-start | bytes 6291460
  67.9 1.4 %copy-start.1 = (bf16[3,2048,128]{2,1,0:T(8,128)(2,1)S(1)}, bf16[3,2048,128]{2,1,0:T(8,128)(2,1)}, u32[]{:S(2)}) copy-start(bf16[3,2048,128]{2,1,0:T(8,128)(2,1)} %weight_ref.1) | copy-start | bytes 4718596

commit v2 on v1

v2 whole, which is shorter than its diff:
```python
import functools

import jax
import jax.numpy as jnp
from jax import lax
from jax.experimental import pallas as pl
from jax.experimental.pallas import tpu as pltpu
from jax.sharding import PartitionSpec as P

BLOCK = 64
HEAD_SIZE = 64
COLS = 2 * HEAD_SIZE
FRAMES = 32
CHUNK = 256
HIDDEN = -16384.0
LOG2E = 1.4426950408889634
MESH = pl.DeviceIdType.MESH
BF16 = jnp.bfloat16
F32 = jnp.float32


def dot(left, right):
    return jnp.dot(left, right, preferred_element_type=F32)


def dot_nt(left, right):
    return lax.dot_general(left, right, (((1,), (1,)), ((), ())), preferred_element_type=F32)


def greet(peers):
    barrier = pltpu.get_barrier_semaphore()
    for peer in peers:
        pl.semaphore_signal(barrier, inc=1, device_id=peer, device_id_type=MESH)
    pl.semaphore_wait(barrier, len(peers))


def remote(source, target, send_sem, recv_sem, peer):
    return pltpu.make_async_remote_copy(
        src_ref=source,
        dst_ref=target,
        send_sem=send_sem,
        recv_sem=recv_sem,
        device_id=peer,
        device_id_type=MESH,
    )


def backward_kernel(
    nz,
    nx,
    frames_hbm,
    stat_hbm,
    query_hbm,
    key_hbm,
    value_hbm,
    out_hbm,
    grad_hbm,
    input_hbm,
    weight_hbm,
    input_out,
    weight_out,
    frames_ref,
    stat_ref,
    query_ref,
    key_ref,
    value_ref,
    out_ref,
    grad_ref,
    input_ref,
    weight_ref,
    key_other,
    value_other,
    slots,
    trail_send,
    trail_recv,
    key_wide,
    value_wide,
    key_flip,
    fixed,
    paired,
    score_low,
    key_sum,
    value_sum,
    early_query,
    part_send,
    part_recv,
    grads_ref,
    flipped_ref,
    core_send,
    core_recv,
    x_send,
    x_recv,
    y_send,
    y_recv,
    zq_send,
    zq_recv,
    zk_send,
    zk_recv,
    yh_send,
    yh_recv,
    load_sems,
    slot_sems,
    trail_sems,
    pair_sems,
    part_sems,
    core_sems,
    x_sems,
    y_sems,
    z_sems,
    yh_sems,
):
    loads = [
        pltpu.make_async_copy(source, target, load_sems.at[i])
        for i, (source, target) in enumerate(
            (
                (grad_hbm, grad_ref),
                (query_hbm, query_ref),
                (out_hbm, out_ref),
                (stat_hbm, stat_ref),
                (key_hbm, key_ref),
                (value_hbm, value_ref),
                (frames_hbm, frames_ref),
                (input_hbm, input_ref),
                (weight_hbm, weight_ref),
            )
        )
    ]
    for load in loads:
        load.start()

    rows = query_ref.shape[0]
    half = rows // 2
    blocks = rows // BLOCK
    count = 2 * nz
    seq = lax.axis_index("seq")
    head = lax.axis_index("head")
    side = lax.rem(seq, 2)
    z = seq // 2
    partner_seq = seq + 1 - 2 * side
    partner = {"seq": partner_seq}
    z_ahead = ({"seq": lax.rem(seq + 2, count)}, {"seq": lax.rem(seq + count - 2, count)})
    core = lax.rem(head, 2)
    x = lax.rem(head // 2, nx)
    low_side = head // (2 * nx)
    twin = {"head": head + 1 - 2 * core}
    plane = low_side * 2 * nx + core
    x_ahead = (
        {"head": plane + 2 * lax.rem(x + 1, nx)},
        {"head": plane + 2 * lax.rem(x + nx - 1, nx)},
    )
    low_head = (1 - low_side) * 2 * nx + 2 * x + core
    neighbour = {"head": low_head}
    y_ahead = (
        {"seq": seq + low_side * (partner_seq - seq), "head": low_head},
        {"seq": partner_seq + low_side * (seq - partner_seq), "head": low_head},
    )
    greet((partner, *z_ahead, twin, *x_ahead, *y_ahead))

    pair_copies = [
        remote(key_hbm, key_other, pair_sems.at[0, 0], pair_sems.at[1, 0], partner),
        remote(value_hbm, value_other, pair_sems.at[0, 1], pair_sems.at[1, 1], partner),
    ]
    for copy in pair_copies:
        copy.start()

    def slot_copy(r, t, part):
        here = pl.ds(0, COLS) if part == 0 else pl.ds(COLS, COLS + 16)
        return remote(
            slots.at[r, t, here],
            slots.at[r, t + 1, here],
            slot_sems.at[0, part, r, t],
            slot_sems.at[1, part, r, t + 1],
            z_ahead[r],
        )

    def trail_copy(r, t):
        return remote(
            trail_send.at[r, t],
            trail_recv.at[r, t + 1],
            trail_sems.at[0, r, t],
            trail_sems.at[1, r, t + 1],
            z_ahead[r],
        )

    for load in loads[:4]:
        load.wait()
    grad_wide = grad_ref[...].astype(F32)
    query_flip = jnp.transpose(query_ref[...].astype(F32) * (HEAD_SIZE**-0.5))
    grad_flip = jnp.transpose(grad_wide)
    delta_flip = jnp.transpose(grad_wide * out_ref[...].astype(F32))
    aux_row = lax.broadcasted_iota(jnp.int32, (16, rows), 0)
    aux = jnp.zeros((16, rows), F32)
    for h in range(2):
        delta = jnp.sum(
            delta_flip[h * HEAD_SIZE : (h + 1) * HEAD_SIZE, :], axis=0, keepdims=True
        )
        for first, value in ((3 * h, stat_ref[h : h + 1, :]), (6 + 3 * h, delta)):
            rest = value
            for place in range(3):
                piece = rest.astype(BF16).astype(F32)
                aux = jnp.where(aux_row == first + place, piece, aux)
                rest = rest - piece
    for r in range(2):
        lanes = slice(r * half, (r + 1) * half)
        slots[r, 0, 0:COLS, :] = query_flip[:, lanes].astype(BF16)
        slots[r, 0, COLS : 2 * COLS, :] = grad_flip[:, lanes].astype(BF16)
        slots[r, 0, 2 * COLS : 2 * COLS + 16, :] = aux[:, lanes].astype(BF16)

    lane = lax.broadcasted_iota(jnp.int32, (BLOCK, COLS), 1)
    inner = lax.rem(lane, HEAD_SIZE)

    def build_keys(keys_from, values_from, base, owner):
        for b in range(blocks):
            here = slice(b * BLOCK, (b + 1) * BLOCK)
            there = slice(base + b * BLOCK, base + (b + 1) * BLOCK)
            frame = frames_ref[owner * blocks + b]
            keys = keys_from[here, :].astype(F32)
            values = values_from[here, :].astype(F32)
            for h in range(2):
                mine = (lane >= h * HEAD_SIZE) & (lane < (h + 1) * HEAD_SIZE)
                stat_at = (inner >= FRAMES + 3 * h) & (inner < FRAMES + 3 * h + 3)
                delta_at = (inner >= FRAMES + 6 + 3 * h) & (inner < FRAMES + 9 + 3 * h)
                key_more = jnp.where(inner == frame, 1.0, jnp.where(stat_at, -1.0, 0.0))
                value_more = jnp.where(delta_at, -1.0, 0.0)
                key_wide[h, there, :] = jnp.where(mine, keys, key_more).astype(BF16)
                value_wide[h, there, :] = jnp.where(mine, values, value_more).astype(BF16)
        key_flip[:, base : base + rows] = jnp.transpose(
            keys_from[...].astype(F32) * (HEAD_SIZE**-0.5)
        ).astype(BF16)

    frame_row = lax.broadcasted_iota(jnp.int32, (FRAMES, half), 0)
    frame_lane = lax.broadcasted_iota(jnp.int32, (FRAMES, half), 1)

    def prepare(t):
        for r, owner in enumerate((lax.rem(seq + 2 * (nz - t), count), lax.rem(seq + 2 * t, count))):
            first = owner * blocks + r * (blocks // 2)
            seen = jnp.full((FRAMES, half), frames_ref[first + blocks // 2 - 1], jnp.int32)
            for i in range(blocks // 2 - 2, -1, -1):
                seen = jnp.where(frame_lane < (i + 1) * BLOCK, frames_ref[first + i], seen)
            hidden = jnp.where(frame_row > seen, HIDDEN, 0.0).astype(BF16)
            extra = jnp.concatenate(
                [hidden, slots[r, t, 2 * COLS : 2 * COLS + 16, :], jnp.zeros((16, half), BF16)],
                axis=0,
            )
            zero = jnp.zeros((HEAD_SIZE, half), BF16)
            for which in range(2):
                low = slots[r, t, which * COLS : which * COLS + HEAD_SIZE, :]
                high = slots[r, t, which * COLS + HEAD_SIZE : (which + 1) * COLS, :]
                fixed[r, 2 * which, :, :] = jnp.concatenate([low, extra], axis=0)
                fixed[r, 2 * which + 1, :, :] = jnp.concatenate([extra, high], axis=0)
                paired[r, which, :, :] = jnp.concatenate(
                    [
                        jnp.concatenate([low, zero], axis=1),
                        jnp.concatenate([zero, high], axis=1),
                    ],
                    axis=0,
                )

    def tile(r, start):
        here = pl.ds(start, CHUNK)
        probs, scores = [], []
        for h in range(2):
            score = dot(key_wide[h, here, :], fixed[r, h, :, :])
            prob = jnp.exp2(score * LOG2E)
            prob_grad = dot(value_wide[h, here, :], fixed[r, 2 + h, :, :])
            score_grad = (prob * prob_grad).astype(BF16)
            score_low[r, h, here, :] = score_grad
            probs.append(prob.astype(BF16))
            scores.append(score_grad)
        value_sum[here, :] += dot_nt(jnp.concatenate(probs, axis=1), paired[r, 1, :, :])
        key_sum[here, :] += dot_nt(jnp.concatenate(scores, axis=1), paired[r, 0, :, :])

    def tiles(first):
        for c in range(rows // CHUNK):
            for r in range(2):
                tile(r, first + c * CHUNK)

    def query_part(r, first, length):
        return jnp.concatenate(
            [
                dot(
                    key_flip[h * HEAD_SIZE : (h + 1) * HEAD_SIZE, first : first + length],
                    score_low[r, h, first : first + length, :],
                )
                for h in range(2)
            ],
            axis=0,
        )

    def receive(t, part):
        for r in range(2):
            slot_copy(r, t - 1, part).wait_recv()

    def forward(t, part):
        for r in range(2):
            slot_copy(r, t, part).start()

    def pass_on(t, part):
        receive(t, part)
        forward(t, part)

    def hand_on(t, totals):
        @pl.when(t > 1)
        def _():
            for r in range(2):
                trail_copy(r, t - 1).wait_recv()

        for r in range(2):
            total = totals[r] + trail_recv[r, t, :, :].astype(F32)
            trail_send[r, t, :, :] = total.astype(BF16)
            trail_copy(r, t).start()

    early = min(3, nz - 1)
    forward(0, 0)
    forward(0, 1)
    for load in loads[4:7]:
        load.wait()
    build_keys(key_ref, value_ref, 0, seq)
    key_sum[...] = jnp.zeros_like(key_sum)
    value_sum[...] = jnp.zeros_like(value_sum)
    for r in range(2):
        trail_recv[r, 1, :, :] = jnp.zeros((COLS, half), BF16)

    def own_step(t, carry):
        @pl.when(t > 0)
        def _():
            pass_on(t, 0)
            pass_on(t, 1)

        prepare(t)
        tiles(0)
        for r in range(2):
            early_query[r, t, :, :] = query_part(r, 0, rows)
        return carry

    lax.fori_loop(0, early, own_step, 0)
    for copy in pair_copies:
        copy.wait()
    build_keys(key_other, value_other, rows, partner_seq)

    def other_step(t, carry):
        prepare(t)
        tiles(rows)
        totals = [early_query[r, t, :, :] + query_part(r, rows, rows) for r in range(2)]

        @pl.when(t == 0)
        def _():
            for r in range(2):
                early_query[r, 0, :, :] = totals[r]

        @pl.when(t > 0)
        def _():
            hand_on(t, totals)

        @pl.when(t == 1)
        def _():
            pass_on(early, 0)
            pass_on(early, 1)

        return carry

    lax.fori_loop(0, early, other_step, 0)

    def step(t, carry):
        @pl.when(t > early)
        def _():
            pass_on(t, 1)

        prepare(t)
        tiles(0)
        tiles(rows)
        receive(t + 1, 0)

        @pl.when(t < nz - 2)
        def _():
            forward(t + 1, 0)

        hand_on(t, [query_part(r, 0, 2 * rows) for r in range(2)])
        return carry

    lax.fori_loop(early, nz - 1, step, 0)
    last = nz - 1
    receive(last, 1)
    prepare(last)
    tiles(rows)
    part_copies = []
    for m, total in enumerate((key_sum, value_sum)):
        part_send[m, :, :] = total[rows:, :].astype(BF16)
        copy = remote(
            part_send.at[m], part_recv.at[m], part_sems.at[0, m], part_sems.at[1, m], partner
        )
        copy.start()
        part_copies.append(copy)
    tiles(0)
    hand_on(last, [query_part(r, 0, 2 * rows) for r in range(2)])
    for load in loads[7:]:
        load.wait()
    started = list(part_copies)

    for r in range(2):
        trail_copy(r, nz - 1).wait_recv()
        lanes = slice(r * half, (r + 1) * half)
        low = (early_query[r, 0, :, :] + trail_recv[r, nz, :, :].astype(F32)).astype(BF16)
        flipped_ref[0:COLS, lanes] = low
        grads_ref[lanes, 0:COLS] = jnp.transpose(low.astype(F32)).astype(BF16)

    def reach(length, i):
        return (length - i) // 2

    def at(r, distance, position, length):
        return lax.rem(position + distance if r == 0 else position + length - distance, length)

    def half_of(r, i):
        return (i + r) % 2

    kinds = (
        (slice(0, COLS), zq_send, zq_recv),
        (slice(COLS, 3 * COLS), zk_send, zk_recv),
    )

    def weight_term(kind, z_at, side_at):
        first = pl.multiple_of((z_at * 2 + side_at) * COLS, COLS)
        return dot(flipped_ref[kinds[kind][0], :], input_ref[:, pl.ds(first, COLS)])

    z_copies = {}

    def z_message(kind, i):
        _, send, recv = kinds[kind]
        for r in range(2):
            total = weight_term(kind, at(r, reach(nz, i), z, nz), half_of(r, i))
            if i >= 2:
                z_copies[kind, r, i - 2].wait_recv()
                total = total + recv[r, i - 2, :, :].astype(F32)
            send[r, i, :, :] = total.astype(BF16)
            copy = remote(
                send.at[r, i],
                recv.at[r, i],
                z_sems.at[kind, 0, r, i],
                z_sems.at[kind, 1, r, i],
                z_ahead[r],
            )
            copy.start()
            z_copies[kind, r, i] = copy
            started.append(copy)

    yh_copies = {}

    def z_final(kind):
        rows_of, _, recv = kinds[kind]
        sides = []
        for side_at in range(2):
            total = weight_term(kind, z, side_at)
            for r in range(2):
                i = nz - 2 if half_of(r, nz - 2) == side_at else nz - 3
                z_copies[kind, r, i].wait_recv()
                total = total + recv[r, i, :, :].astype(F32)
            sides.append(total)
        yh_send[rows_of, :] = jnp.where(side == 0, sides[1], sides[0]).astype(BF16)
        copy = remote(
            yh_send.at[rows_of],
            yh_recv.at[rows_of],
            yh_sems.at[0, kind],
            yh_sems.at[1, kind],
            partner,
        )
        copy.start()
        yh_copies[kind] = copy
        started.append(copy)
        return jnp.where(side == 0, sides[0], sides[1])

    def weight_done(kind, kept):
        rows_of, _, _ = kinds[kind]
        yh_copies[kind].wait_recv()
        total = kept + yh_recv[rows_of, :].astype(F32)
        for place in range(total.shape[0] // COLS):
            m = rows_of.start // COLS + place
            weight_out[m, :, :] = jnp.transpose(total[place * COLS : (place + 1) * COLS, :])

    def input_term(x_at, y_at, core_at):
        first = pl.multiple_of(((y_at * nx + x_at) * 2 + core_at) * COLS, COLS)
        weights = jnp.concatenate(
            [weight_ref[m, pl.ds(first, COLS), :] for m in range(3)], axis=1
        )
        return dot_nt(grads_ref[...], weights)

    core_order = [(r, i) for i in range(nx - 1) for r in range(2)] + [(0, nx - 1), (0, nx)]
    core_copies = {}

    def core_message(place):
        r, i = core_order[place]
        term = input_term(at(r, reach(nx, i), x, nx), half_of(r, i), 1 - core)
        core_send[place, :, :] = term.astype(BF16)
        copy = remote(
            core_send.at[place],
            core_recv.at[place],
            core_sems.at[0, place],
            core_sems.at[1, place],
            twin,
        )
        copy.start()
        core_copies[r, i] = (place, copy)
        started.append(copy)

    x_copies = {}

    def input_pair(r, i):
        place, copy = core_copies[r, i]
        total = input_term(at(r, reach(nx, i), x, nx), half_of(r, i), core)
        copy.wait_recv()
        return total + core_recv[place, :, :].astype(F32)

    def x_message(i):
        for r in range(2):
            total = input_pair(r, i)
            if i >= 2:
                x_copies[r, i - 2].wait_recv()
                total = total + x_recv[r, i - 2, :, :].astype(F32)
            x_send[r, i, :, :] = total.astype(BF16)
            copy = remote(
                x_send.at[r, i], x_recv.at[r, i], x_sems.at[0, r, i], x_sems.at[1, r, i], x_ahead[r]
            )
            copy.start()
            x_copies[r, i] = copy
            started.append(copy)

    def x_final(place):
        total = input_pair(0, nx - 1 + place)
        y_at = half_of(0, nx - 1 + place)
        for r in range(2):
            i = nx - 2 if half_of(r, nx - 2) == y_at else nx - 3
            x_copies[r, i].wait_recv()
            total = total + x_recv[r, i, :, :].astype(F32)
        return y_at, total

    z_message(0, 0)
    z_message(0, 1)
    for m, total in ((1, key_sum), (2, value_sum)):
        part_copies[m - 1].wait_recv()
        low = (total[0:rows, :] + part_recv[m - 1, :, :].astype(F32)).astype(BF16)
        grads_ref[:, m * COLS : (m + 1) * COLS] = low
        flipped_ref[m * COLS : (m + 1) * COLS, :] = jnp.transpose(low.astype(F32)).astype(BF16)
    z_message(1, 0)
    for place in range(4):
        core_message(place)
    z_message(1, 1)
    z_message(0, 2)
    x_message(0)
    for place in range(4, 2 * nx):
        core_message(place)
    x_message(1)
    z_message(0, 3)
    z_message(1, 2)
    z_message(0, 4)
    z_message(1, 3)
    z_message(0, 5)
    x_message(2)
    z_message(1, 4)
    z_message(0, 6)
    finals = dict(x_final(place) for place in range(2))
    y_send[...] = jnp.where(low_side == 0, finals[1], finals[0]).astype(BF16)
    y_copy = remote(y_send, y_recv, y_sems.at[0], y_sems.at[1], neighbour)
    y_copy.start()
    mine = jnp.where(low_side == 0, finals[0], finals[1])
    z_message(1, 5)
    kept_query = z_final(0)
    z_message(1, 6)
    kept_key = z_final(1)
    y_copy.wait_recv()
    input_out[...] = (mine + y_recv[...].astype(F32)).astype(BF16)
    weight_done(0, kept_query)
    weight_done(1, kept_key)
    y_copy.wait_send()
    for copy in started:
        copy.wait_send()
    for r in range(2):

        def drain(t, carry, r=r):
            slot_copy(r, t, 0).wait_send()
            slot_copy(r, t, 1).wait_send()
            trail_copy(r, t + 1).wait_send()
            return carry

        lax.fori_loop(0, nz - 1, drain, 0)


def local(
    nz,
    nx,
    layer_input,
    qkv_weight,
    queries,
    key_states,
    value_states,
    attn_out,
    grad_out,
    log_sum_exp,
    frames,
):
    rows = queries.shape[0]
    half = rows // 2
    wide = 3 * COLS
    vmem = pl.BlockSpec(memory_space=pltpu.VMEM)
    anywhere = pl.BlockSpec(memory_space=pl.ANY)
    dma = pltpu.SemaphoreType.DMA
    stat = log_sum_exp.T

    def low(*shape):
        return pltpu.VMEM(shape, BF16)

    def full(*shape):
        return pltpu.VMEM(shape, F32)

    return pl.pallas_call(
        functools.partial(backward_kernel, nz, nx),
        out_shape=(
            jax.ShapeDtypeStruct((rows, COLS), BF16),
            jax.ShapeDtypeStruct((3, COLS, COLS), F32),
        ),
        in_specs=[anywhere] * 9,
        out_specs=(vmem, vmem),
        scratch_shapes=[
            pltpu.SMEM(frames.shape, jnp.int32),
            full(*stat.shape),
            low(rows, COLS),
            low(rows, COLS),
            low(rows, COLS),
            low(rows, COLS),
            low(rows, COLS),
            low(*layer_input.shape),
            low(*qkv_weight.shape),
            low(rows, COLS),
            low(rows, COLS),
            low(2, nz, 2 * COLS + 16, half),
            low(2, nz, COLS, half),
            low(2, nz + 1, COLS, half),
            low(2, 2 * rows, COLS),
            low(2, 2 * rows, COLS),
            low(COLS, 2 * rows),
            low(2, 4, COLS, half),
            low(2, 2, COLS, 2 * half),
            low(2, 2, 2 * rows, half),
            full(2 * rows, COLS),
            full(2 * rows, COLS),
            full(2, 3, COLS, half),
            low(2, rows, COLS),
            low(2, rows, COLS),
            low(rows, wide),
            low(wide, rows),
            low(2 * nx, rows, COLS),
            low(2 * nx, rows, COLS),
            low(2, nx - 1, rows, COLS),
            low(2, nx - 1, rows, COLS),
            low(rows, COLS),
            low(rows, COLS),
            low(2, nz - 1, COLS, COLS),
            low(2, nz - 1, COLS, COLS),
            low(2, nz - 1, 2 * COLS, COLS),
            low(2, nz - 1, 2 * COLS, COLS),
            low(wide, COLS),
            low(wide, COLS),
            dma((9,)),
            dma((2, 2, 2, nz)),
            dma((2, 2, nz + 1)),
            dma((2, 2)),
            dma((2, 2)),
            dma((2, 2 * nx)),
            dma((2, 2, nx - 1)),
            dma((2,)),
            dma((2, 2, 2, nz - 1)),
            dma((2, 2)),
        ],
        compiler_params=pltpu.CompilerParams(
            collective_id=0, has_side_effects=True, vmem_limit_bytes=56 * 2**20
        ),
        name="attention_backward",
    )(
        frames,
        stat,
        queries,
        key_states,
        value_states,
        attn_out,
        grad_out,
        layer_input,
        qkv_weight,
    )


def solution(mesh):
    nz = mesh.shape["seq"] // 2
    nx = mesh.shape["head"] // 4
    placed = (
        P("seq", None),
        P(None, None, "head"),
        P("seq", "head"),
        P("seq", "head"),
        P("seq", "head"),
        P("seq", "head"),
        P("seq", "head"),
        P("seq", "head"),
        P(),
    )
    return jax.shard_map(
        functools.partial(local, nz, nx),
        mesh=mesh,
        in_specs=placed,
        out_specs=(P("seq", "head"), P(None, "seq", "head")),
        check_vma=False,
    )
```

time: 102 us -> 84.6 us (0.83)
  Pallas kernels: 90.6 us -> 80.1 us
  local copies, waits for them, and re-layouts: 10.2 us -> 3.18 us
    pallas_call x2 -> x1, Pallas kernels: 90.6 us -> 80.1 us  [local(): pl.pallas_call(functools.partial(backward_kernel, nz, nx), out_shape=(jax...]
    unnamed x20 -> x2, local copies, waits for them, and re-layouts: 10.2 us -> 3.18 us
where the time goes in v2:
time: 84.6 us; the launch traced here: 84 us
  Pallas kernels  80.1 us (95%)
  local copies, waits for them, and re-layouts  3.18 us (4%)
    pallas_call x1, Pallas kernels, local(): pl.pallas_call(functools.partial(backward_kernel, nz, nx), out_shape=(jax...  80.1 us
    unnamed x2, local copies, waits for them, and re-layouts  3.18 us

profile of v2, /device:TPU:2, one launch (start us, length us, event | category | flops | bytes accessed | tf_op | source)
XLA Modules:
  0.0 84.0 jit_solution(9232228865887137170)
XLA Ops:
  0.6 80.1 %attention_backward.1 = (bf16[512,128]{1,0:T(8,128)(2,1)}, f32[3,128,128]{2,1,0:T(8,128)}) custom-call(s32[128]{0:T(128)} %frames_hbm.1, f32[2,512]{1,0:T(2,128)} %bitcast.1, bf16[512,128]{1,0:T(8,128)(2,1)} %query_hbm.1, bf16[512,128]{1,0:T(8,128)(2,1)} %key_hbm.1, bf16[512,128]{1,0:T(8,128)(2,1)} %value_hbm.1, bf16[512,128]{1,0:T(8,128)(2,1)} %out_hbm.1, ...), custom_call_target="tpu_custom_call" | custom-call | tf_op jit(solution)/shard_map/attention_backward/pallas_call | solution.py:613
  80.8 1.6 %copy.13 = bf16[512,128]{1,0:T(8,128)(2,1)} copy(bf16[512,128]{1,0:T(8,128)(2,1)} %get-tuple-element.4) | data formatting | bytes 262144
  82.3 1.6 %copy.14 = f32[3,128,128]{2,1,0:T(8,128)} copy(f32[3,128,128]{2,1,0:T(8,128)} %get-tuple-element.5) | data formatting | bytes 393216

commit v3 on v2

--- a/solution.py
+++ b/solution.py
@@ -15,6 +15,7 @@
 HIDDEN = -16384.0
 LOG2E = 1.4426950408889634
 MESH = pl.DeviceIdType.MESH
+PIECES = (0, 128, 272)
 BF16 = jnp.bfloat16
 F32 = jnp.float32
 
@@ -90,14 +91,21 @@
     core_recv,
     x_send,
     x_recv,
+    x_term,
+    own_term,
     y_send,
     y_recv,
+    zq_term,
     zq_send,
     zq_recv,
+    zq_last,
+    zk_term,
     zk_send,
     zk_recv,
-    yh_send,
-    yh_recv,
+    zk_last,
+    near_term,
+    near_send,
+    near_recv,
     load_sems,
     slot_sems,
     trail_sems,
@@ -107,7 +115,8 @@
     x_sems,
     y_sems,
     z_sems,
-    yh_sems,
+    last_sems,
+    near_sems,
 ):
     loads = [
         pltpu.make_async_copy(source, target, load_sems.at[i])
@@ -148,13 +157,9 @@
         {"head": plane + 2 * lax.rem(x + 1, nx)},
         {"head": plane + 2 * lax.rem(x + nx - 1, nx)},
     )
-    low_head = (1 - low_side) * 2 * nx + 2 * x + core
-    neighbour = {"head": low_head}
-    y_ahead = (
-        {"seq": seq + low_side * (partner_seq - seq), "head": low_head},
-        {"seq": partner_seq + low_side * (seq - partner_seq), "head": low_head},
-    )
-    greet((partner, *z_ahead, twin, *x_ahead, *y_ahead))
+    neighbour = {"head": (1 - low_side) * 2 * nx + 2 * x + core}
+    slants = [{"seq": 2 * lax.rem(z + dz, nz) + 1 - side} for dz in (1, nz - 1)]
+    greet((partner, *z_ahead, *slants, twin, neighbour, *x_ahead))
 
     pair_copies = [
         remote(key_hbm, key_other, pair_sems.at[0, 0], pair_sems.at[1, 0], partner),
@@ -164,7 +169,7 @@
         copy.start()
 
     def slot_copy(r, t, part):
-        here = pl.ds(0, COLS) if part == 0 else pl.ds(COLS, COLS + 16)
+        here = pl.ds(PIECES[part], PIECES[part + 1] - PIECES[part])
         return remote(
             slots.at[r, t, here],
             slots.at[r, t + 1, here],
@@ -287,17 +292,23 @@
             axis=0,
         )
 
-    def receive(t, part):
-        for r in range(2):
-            slot_copy(r, t - 1, part).wait_recv()
+    every = range(len(PIECES) - 1)
 
     def forward(t, part):
         for r in range(2):
             slot_copy(r, t, part).start()
 
-    def pass_on(t, part):
-        receive(t, part)
-        forward(t, part)
+    def pass_on(t, parts):
+        for part in parts:
+            for r in range(2):
+                slot_copy(r, t - 1, part).wait_recv()
+
+            if isinstance(t, int):
+                continue
+
+            @pl.when(t < nz - 1)
+            def _(part=part):
+                forward(t, part)
 
     def hand_on(t, totals):
         @pl.when(t > 1)
@@ -310,9 +321,9 @@
             trail_send[r, t, :, :] = total.astype(BF16)
             trail_copy(r, t).start()
 
-    early = min(3, nz - 1)
-    forward(0, 0)
-    forward(0, 1)
+    early = min(2, nz - 1)
+    for part in every:
+        forward(0, part)
     for load in loads[4:7]:
         load.wait()
     build_keys(key_ref, value_ref, 0, seq)
@@ -324,8 +335,7 @@
     def own_step(t, carry):
         @pl.when(t > 0)
         def _():
-            pass_on(t, 0)
-            pass_on(t, 1)
+            pass_on(t, every)
 
         prepare(t)
         tiles(0)
@@ -352,10 +362,9 @@
         def _():
             hand_on(t, totals)
 
-        @pl.when(t == 1)
+        @pl.when(t == 0)
         def _():
-            pass_on(early, 0)
-            pass_on(early, 1)
+            pass_on(t + early - 0, every)
 
         return carry
 
@@ -364,23 +373,20 @@
     def step(t, carry):
         @pl.when(t > early)
         def _():
-            pass_on(t, 1)
+            pass_on(t, every[1:])
 
         prepare(t)
         tiles(0)
         tiles(rows)
-        receive(t + 1, 0)
-
-        @pl.when(t < nz - 2)
-        def _():
-            forward(t + 1, 0)
-
+        pass_on(t + 1, every[:1])
         hand_on(t, [query_part(r, 0, 2 * rows) for r in range(2)])
         return carry
 
     lax.fori_loop(early, nz - 1, step, 0)
     last = nz - 1
-    receive(last, 1)
+    for load in loads[7:]:
+        load.wait()
+    pass_on(last, every[1:])
     prepare(last)
     tiles(rows)
     part_copies = []
@@ -393,8 +399,6 @@
         part_copies.append(copy)
     tiles(0)
     hand_on(last, [query_part(r, 0, 2 * rows) for r in range(2)])
-    for load in loads[7:]:
-        load.wait()
     started = list(part_copies)
 
     for r in range(2):
@@ -404,183 +408,214 @@
         flipped_ref[0:COLS, lanes] = low
         grads_ref[lanes, 0:COLS] = jnp.transpose(low.astype(F32)).astype(BF16)
 
-    def reach(length, i):
-        return (length - i) // 2
-
-    def at(r, distance, position, length):
-        return lax.rem(position + distance if r == 0 else position + length - distance, length)
+    def launch(copy):
+        copy.start()
+        started.append(copy)
+        return copy
+
+    def at(r, distance):
+        return lax.rem(z + distance if r == 0 else z + nz - distance, nz)
 
     def half_of(r, i):
         return (i + r) % 2
 
     kinds = (
-        (slice(0, COLS), zq_send, zq_recv),
-        (slice(COLS, 3 * COLS), zk_send, zk_recv),
+        (slice(0, COLS), zq_term, zq_send, zq_recv, zq_last),
+        (slice(COLS, 3 * COLS), zk_term, zk_send, zk_recv, zk_last),
     )
+    z_copies = {}
 
     def weight_term(kind, z_at, side_at):
         first = pl.multiple_of((z_at * 2 + side_at) * COLS, COLS)
         return dot(flipped_ref[kinds[kind][0], :], input_ref[:, pl.ds(first, COLS)])
 
-    z_copies = {}
-
-    def z_message(kind, i):
-        _, send, recv = kinds[kind]
+    def z_term(kind, i):
         for r in range(2):
-            total = weight_term(kind, at(r, reach(nz, i), z, nz), half_of(r, i))
+            kinds[kind][1][r, i, :, :] = weight_term(kind, at(r, (nz - i) // 2), half_of(r, i))
+
+    def z_message(kind, i, ready=False):
+        _, term, send, recv, final = kinds[kind]
+        if not ready:
+            z_term(kind, i)
+        for r in range(2):
+            total = term[r, i, :, :]
             if i >= 2:
                 z_copies[kind, r, i - 2].wait_recv()
                 total = total + recv[r, i - 2, :, :].astype(F32)
             send[r, i, :, :] = total.astype(BF16)
-            copy = remote(
-                send.at[r, i],
-                recv.at[r, i],
-                z_sems.at[kind, 0, r, i],
-                z_sems.at[kind, 1, r, i],
-                z_ahead[r],
+            if i < nz - 3:
+                copy = remote(
+                    send.at[r, i],
+                    recv.at[r, i],
+                    z_sems.at[kind, 0, r, i],
+                    z_sems.at[kind, 1, r, i],
+                    z_ahead[r],
+                )
+            else:
+                copy = remote(
+                    send.at[r, i],
+                    final.at[r, side],
+                    z_sems.at[kind, 0, r, i],
+                    last_sems.at[kind, r, side],
+                    {"seq": 2 * at(r, 1) + half_of(r, i)},
+                )
+            z_copies[kind, r, i] = launch(copy)
+
+    near_copies = {}
+
+    def z_near(kind):
+        rows_of = kinds[kind][0]
+        near_send[rows_of, :] = weight_term(kind, z, 1 - side).astype(BF16)
+        near_copies[kind] = launch(
+            remote(
+                near_send.at[rows_of],
+                near_recv.at[rows_of],
+                near_sems.at[0, kind],
+                near_sems.at[1, kind],
+                partner,
             )
-            copy.start()
-            z_copies[kind, r, i] = copy
-            started.append(copy)
-
-    yh_copies = {}
+        )
+        near_term[rows_of, :] = weight_term(kind, z, side)
 
     def z_final(kind):
-        rows_of, _, recv = kinds[kind]
-        sides = []
-        for side_at in range(2):
-            total = weight_term(kind, z, side_at)
-            for r in range(2):
-                i = nz - 2 if half_of(r, nz - 2) == side_at else nz - 3
-                z_copies[kind, r, i].wait_recv()
-                total = total + recv[r, i, :, :].astype(F32)
-            sides.append(total)
-        yh_send[rows_of, :] = jnp.where(side == 0, sides[1], sides[0]).astype(BF16)
-        copy = remote(
-            yh_send.at[rows_of],
-            yh_recv.at[rows_of],
-            yh_sems.at[0, kind],
-            yh_sems.at[1, kind],
-            partner,
-        )
-        copy.start()
-        yh_copies[kind] = copy
-        started.append(copy)
-        return jnp.where(side == 0, sides[0], sides[1])
-
-    def weight_done(kind, kept):
-        rows_of, _, _ = kinds[kind]
-        yh_copies[kind].wait_recv()
-        total = kept + yh_recv[rows_of, :].astype(F32)
+        rows_of, _, send, _, final = kinds[kind]
+        near_copies[kind].wait_recv()
+        total = near_term[rows_of, :] + near_recv[rows_of, :].astype(F32)
+        for r in range(2):
+            for source in range(2):
+                remote(
+                    send.at[r, 0],
+                    final.at[r, source],
+                    z_sems.at[kind, 0, r, 0],
+                    last_sems.at[kind, r, source],
+                    partner,
+                ).wait_recv()
+                total = total + final[r, source, :, :].astype(F32)
         for place in range(total.shape[0] // COLS):
             m = rows_of.start // COLS + place
             weight_out[m, :, :] = jnp.transpose(total[place * COLS : (place + 1) * COLS, :])
 
-    def input_term(x_at, y_at, core_at):
-        first = pl.multiple_of(((y_at * nx + x_at) * 2 + core_at) * COLS, COLS)
-        weights = jnp.concatenate(
-            [weight_ref[m, pl.ds(first, COLS), :] for m in range(3)], axis=1
-        )
-        return dot_nt(grads_ref[...], weights)
-
-    core_order = [(r, i) for i in range(nx - 1) for r in range(2)] + [(0, nx - 1), (0, nx)]
+    def input_term(dx, core_at):
+        weights = []
+        for y_at in range(2):
+            first = pl.multiple_of(((y_at * nx + lax.rem(x + dx, nx)) * 2 + core_at) * COLS, COLS)
+            weights.append(
+                jnp.concatenate([weight_ref[m, pl.ds(first, COLS), :] for m in range(3)], axis=1)
+            )
+        return dot_nt(grads_ref[...], jnp.concatenate(weights, axis=0))
+
     core_copies = {}
 
-    def core_message(place):
-        r, i = core_order[place]
-        term = input_term(at(r, reach(nx, i), x, nx), half_of(r, i), 1 - core)
-        core_send[place, :, :] = term.astype(BF16)
-        copy = remote(
-            core_send.at[place],
-            core_recv.at[place],
-            core_sems.at[0, place],
-            core_sems.at[1, place],
-            twin,
-        )
-        copy.start()
-        core_copies[r, i] = (place, copy)
-        started.append(copy)
+    def core_message(dx):
+        core_send[dx, :, :] = input_term(dx, 1 - core).astype(BF16)
+        core_copies[dx] = launch(
+            remote(
+                core_send.at[dx],
+                core_recv.at[dx],
+                core_sems.at[0, dx],
+                core_sems.at[1, dx],
+                twin,
+            )
+        )
 
     x_copies = {}
 
-    def input_pair(r, i):
-        place, copy = core_copies[r, i]
-        total = input_term(at(r, reach(nx, i), x, nx), half_of(r, i), core)
-        copy.wait_recv()
-        return total + core_recv[place, :, :].astype(F32)
-
-    def x_message(i):
-        for r in range(2):
-            total = input_pair(r, i)
-            if i >= 2:
-                x_copies[r, i - 2].wait_recv()
-                total = total + x_recv[r, i - 2, :, :].astype(F32)
+    def x_message(r, i):
+        if i >= 2:
+            x_copies[r, i - 2].wait_recv()
+            total = x_term[r, :, :] + x_recv[r, i - 2, :, :].astype(F32)
             x_send[r, i, :, :] = total.astype(BF16)
-            copy = remote(
+        x_copies[r, i] = launch(
+            remote(
                 x_send.at[r, i], x_recv.at[r, i], x_sems.at[0, r, i], x_sems.at[1, r, i], x_ahead[r]
             )
-            copy.start()
-            x_copies[r, i] = copy
-            started.append(copy)
-
-    def x_final(place):
-        total = input_pair(0, nx - 1 + place)
-        y_at = half_of(0, nx - 1 + place)
+        )
+
+    def input_pair(dx):
+        total = input_term(dx, core)
+        core_copies[dx].wait_recv()
+        total = total + core_recv[dx, :, :].astype(F32)
+        return [total[:, y_at * COLS : (y_at + 1) * COLS] for y_at in range(2)]
+
+    def x_first():
+        sides = input_pair(2)
         for r in range(2):
-            i = nx - 2 if half_of(r, nx - 2) == y_at else nx - 3
-            x_copies[r, i].wait_recv()
-            total = total + x_recv[r, i, :, :].astype(F32)
-        return y_at, total
+            x_send[r, 0, :, :] = sides[r].astype(BF16)
+            x_message(r, 0)
+
+    def x_second(r):
+        sides = input_pair(1 if r == 0 else nx - 1)
+        x_send[r, 1, :, :] = sides[1 - r].astype(BF16)
+        x_message(r, 1)
+        x_term[r, :, :] = sides[r]
+
+    def x_own():
+        for y_at, total in enumerate(input_pair(0)):
+            own_term[y_at, :, :] = total
+
+    def x_final():
+        totals = []
+        for y_at in range(2):
+            total = own_term[y_at, :, :]
+            for r in range(2):
+                i = 2 if r == y_at else 1
+                x_copies[r, i].wait_recv()
+                total = total + x_recv[r, i, :, :].astype(F32)
+            totals.append(total)
+        y_send[...] = jnp.where(low_side == 0, totals[1], totals[0]).astype(BF16)
+        own_term[0, :, :] = jnp.where(low_side == 0, totals[0], totals[1])
+        return launch(remote(y_send, y_recv, y_sems.at[0], y_sems.at[1], neighbour))
+
+    def drain(t, carry):
+        for r in range(2):
+            for part in every:
+                slot_copy(r, t, part).wait_send()
+            trail_copy(r, t + 1).wait_send()
+        return carry
 
     z_message(0, 0)
     z_message(0, 1)
+    z_near(0)
+    for i in range(2, nz - 1):
+        z_term(0, i)
+    lax.fori_loop(0, nz - 1, drain, 0)
     for m, total in ((1, key_sum), (2, value_sum)):
         part_copies[m - 1].wait_recv()
         low = (total[0:rows, :] + part_recv[m - 1, :, :].astype(F32)).astype(BF16)
         grads_ref[:, m * COLS : (m + 1) * COLS] = low
         flipped_ref[m * COLS : (m + 1) * COLS, :] = jnp.transpose(low.astype(F32)).astype(BF16)
     z_message(1, 0)
-    for place in range(4):
-        core_message(place)
+    core_message(2)
     z_message(1, 1)
-    z_message(0, 2)
-    x_message(0)
-    for place in range(4, 2 * nx):
-        core_message(place)
-    x_message(1)
-    z_message(0, 3)
+    core_message(1)
+    z_message(0, 2, True)
+    z_message(0, 3, True)
+    x_first()
+    core_message(3)
+    x_second(0)
+    core_message(0)
+    x_second(1)
     z_message(1, 2)
-    z_message(0, 4)
     z_message(1, 3)
-    z_message(0, 5)
-    x_message(2)
-    z_message(1, 4)
-    z_message(0, 6)
-    finals = dict(x_final(place) for place in range(2))
-    y_send[...] = jnp.where(low_side == 0, finals[1], finals[0]).astype(BF16)
-    y_copy = remote(y_send, y_recv, y_sems.at[0], y_sems.at[1], neighbour)
-    y_copy.start()
-    mine = jnp.where(low_side == 0, finals[0], finals[1])
-    z_message(1, 5)
-    kept_query = z_final(0)
-    z_message(1, 6)
-    kept_key = z_final(1)
+    z_message(0, 4, True)
+    z_message(0, 5, True)
+    x_own()
+    z_near(1)
+    for i in range(4, nz - 1):
+        z_term(1, i)
+    x_message(0, 2)
+    x_message(1, 2)
+    z_message(1, 4, True)
+    z_message(1, 5, True)
+    z_message(0, 6, True)
+    z_message(1, 6, True)
+    z_final(0)
+    y_copy = x_final()
+    z_final(1)
     y_copy.wait_recv()
-    input_out[...] = (mine + y_recv[...].astype(F32)).astype(BF16)
-    weight_done(0, kept_query)
-    weight_done(1, kept_key)
-    y_copy.wait_send()
+    input_out[...] = (own_term[0, :, :] + y_recv[...].astype(F32)).astype(BF16)
     for copy in started:
         copy.wait_send()
-    for r in range(2):
-
-        def drain(t, carry, r=r):
-            slot_copy(r, t, 0).wait_send()
-            slot_copy(r, t, 1).wait_send()
-            trail_copy(r, t + 1).wait_send()
-            return carry
-
-        lax.fori_loop(0, nz - 1, drain, 0)
 
 
 def local(
@@ -600,7 +635,7 @@
     half = rows // 2
     wide = 3 * COLS
     vmem = pl.BlockSpec(memory_space=pltpu.VMEM)
-    anywhere = pl.BlockSpec(memory_space=pl.ANY)
+    anywhere = pl.BlockSpec(memory_space=pltpu.HBM)
     dma = pltpu.SemaphoreType.DMA
     stat = log_sum_exp.T
 
@@ -613,8 +648,8 @@
     return pl.pallas_call(
         functools.partial(backward_kernel, nz, nx),
         out_shape=(
-            jax.ShapeDtypeStruct((rows, COLS), BF16),
-            jax.ShapeDtypeStruct((3, COLS, COLS), F32),
+            pltpu.VMEM((rows, COLS), BF16),
+            pltpu.VMEM((3, COLS, COLS), F32),
         ),
         in_specs=[anywhere] * 9,
         out_specs=(vmem, vmem),
@@ -641,48 +676,61 @@
             low(2, 2, 2 * rows, half),
             full(2 * rows, COLS),
             full(2 * rows, COLS),
-            full(2, 3, COLS, half),
+            full(2, 2, COLS, half),
             low(2, rows, COLS),
             low(2, rows, COLS),
             low(rows, wide),
             low(wide, rows),
-            low(2 * nx, rows, COLS),
-            low(2 * nx, rows, COLS),
-            low(2, nx - 1, rows, COLS),
-            low(2, nx - 1, rows, COLS),
-            low(rows, COLS),
-            low(rows, COLS),
+            low(nx, rows, 2 * COLS),
+            low(nx, rows, 2 * COLS),
+            low(2, 3, rows, COLS),
+            low(2, 3, rows, COLS),
+            full(2, rows, COLS),
+            full(2, rows, COLS),
+            low(rows, COLS),
+            low(rows, COLS),
+            full(2, nz - 1, COLS, COLS),
             low(2, nz - 1, COLS, COLS),
-            low(2, nz - 1, COLS, COLS),
+            low(2, nz - 3, COLS, COLS),
+            low(2, 2, COLS, COLS),
+            full(2, nz - 1, 2 * COLS, COLS),
             low(2, nz - 1, 2 * COLS, COLS),
-            low(2, nz - 1, 2 * COLS, COLS),
+            low(2, nz - 3, 2 * COLS, COLS),
+            low(2, 2, 2 * COLS, COLS),
+            full(wide, COLS),
             low(wide, COLS),
             low(wide, COLS),
             dma((9,)),
-            dma((2, 2, 2, nz)),
+            dma((2, len(PIECES) - 1, 2, nz)),
             dma((2, 2, nz + 1)),
             dma((2, 2)),
             dma((2, 2)),
-            dma((2, 2 * nx)),
-            dma((2, 2, nx - 1)),
+            dma((2, nx)),
+            dma((2, 2, 3)),
             dma((2,)),
             dma((2, 2, 2, nz - 1)),
+            dma((2, 2, 2)),
             dma((2, 2)),
         ],
         compiler_params=pltpu.CompilerParams(
-            collective_id=0, has_side_effects=True, vmem_limit_bytes=56 * 2**20
+            collective_id=0, has_side_effects=True, vmem_limit_bytes=48 * 2**20
         ),
         name="attention_backward",
     )(
-        frames,
-        stat,
-        queries,
-        key_states,
-        value_states,
-        attn_out,
-        grad_out,
-        layer_input,
-        qkv_weight,
+        *(
+            pltpu.with_memory_space_constraint(array, pltpu.HBM)
+            for array in (
+                frames,
+                stat,
+                queries,
+                key_states,
+                value_states,
+                attn_out,
+                grad_out,
+                layer_input,
+                qkv_weight,
+            )
+        )
     )
 
 

time: 84.6 us -> 78.8 us (0.931)
  Pallas kernels: 80.1 us -> 76.8 us
  local copies, waits for them, and re-layouts: 3.18 us -> 1.33 us
    pallas_call x1, Pallas kernels: 80.1 us -> 76.8 us  [local(): pl.pallas_call(functools.partial(backward_kernel, nz, nx), out_shape=(plt...]
    unnamed x2, local copies, waits for them, and re-layouts: 3.18 us -> 1.33 us
where the time goes in v3:
time: 78.8 us; the launch traced here: 78.7 us
  Pallas kernels  76.8 us (97%)
  local copies, waits for them, and re-layouts  1.33 us (2%)
    pallas_call x1, Pallas kernels, local(): pl.pallas_call(functools.partial(backward_kernel, nz, nx), out_shape=(plt...  76.8 us

profile of v3, /device:TPU:2, one launch (start us, length us, event | category | flops | bytes accessed | tf_op | source)
XLA Modules:
  0.0 78.7 jit_solution(10719655765696149465)
XLA Ops:
  0.6 76.8 %attention_backward.1 = (bf16[512,128]{1,0:T(8,128)(2,1)S(1)}, f32[3,128,128]{2,1,0:T(8,128)S(1)}) custom-call(s32[128]{0:T(128)} %frames_hbm.1, f32[2,512]{1,0:T(2,128)} %bitcast.1, bf16[512,128]{1,0:T(8,128)(2,1)} %query_hbm.1, bf16[512,128]{1,0:T(8,128)(2,1)} %key_hbm.1, bf16[512,128]{1,0:T(8,128)(2,1)} %value_hbm.1, bf16[512,128]{1,0:T(8,128)(2,1)} %out_hbm.1, ...), custom_call_target="tpu_custom_call" | custom-call | tf_op jit(solution)/shard_map/attention_backward/pallas_call | solution.py:648
  77.4 0.7 copy.13
  78.1 0.7 copy.14

commit v4 on v3

--- a/solution.py
+++ b/solution.py
@@ -32,7 +32,6 @@
     barrier = pltpu.get_barrier_semaphore()
     for peer in peers:
         pl.semaphore_signal(barrier, inc=1, device_id=peer, device_id_type=MESH)
-    pl.semaphore_wait(barrier, len(peers))
 
 
 def remote(source, target, send_sem, recv_sem, peer):
@@ -89,12 +88,17 @@
     flipped_ref,
     core_send,
     core_recv,
-    x_send,
-    x_recv,
-    x_term,
-    own_term,
-    y_send,
-    y_recv,
+    xa_send,
+    xa_recv,
+    xa_term,
+    xa_own,
+    xb_send,
+    xb_recv,
+    yb_send,
+    yb_recv,
+    yb_term,
+    ya_send,
+    ya_recv,
     zq_term,
     zq_send,
     zq_recv,
@@ -112,7 +116,8 @@
     pair_sems,
     part_sems,
     core_sems,
-    x_sems,
+    xa_sems,
+    xb_sems,
     y_sems,
     z_sems,
     last_sems,
@@ -122,8 +127,8 @@
         pltpu.make_async_copy(source, target, load_sems.at[i])
         for i, (source, target) in enumerate(
             (
+                (query_hbm, query_ref),
                 (grad_hbm, grad_ref),
-                (query_hbm, query_ref),
                 (out_hbm, out_ref),
                 (stat_hbm, stat_ref),
                 (key_hbm, key_ref),
@@ -159,15 +164,13 @@
     )
     neighbour = {"head": (1 - low_side) * 2 * nx + 2 * x + core}
     slants = [{"seq": 2 * lax.rem(z + dz, nz) + 1 - side} for dz in (1, nz - 1)]
-    greet((partner, *z_ahead, *slants, twin, neighbour, *x_ahead))
+    peers = (*z_ahead, partner, *slants, twin, neighbour, *x_ahead)
+    greet(peers)
 
     pair_copies = [
         remote(key_hbm, key_other, pair_sems.at[0, 0], pair_sems.at[1, 0], partner),
         remote(value_hbm, value_other, pair_sems.at[0, 1], pair_sems.at[1, 1], partner),
     ]
-    for copy in pair_copies:
-        copy.start()
-
     def slot_copy(r, t, part):
         here = pl.ds(PIECES[part], PIECES[part + 1] - PIECES[part])
         return remote(
@@ -187,10 +190,23 @@
             z_ahead[r],
         )
 
-    for load in loads[:4]:
+    every = range(len(PIECES) - 1)
+
+    def forward(t, part):
+        for r in range(2):
+            slot_copy(r, t, part).start()
+
+    loads[0].wait()
+    query_flip = jnp.transpose(query_ref[...].astype(F32) * (HEAD_SIZE**-0.5))
+    for r in range(2):
+        slots[r, 0, 0:COLS, :] = query_flip[:, r * half : (r + 1) * half].astype(BF16)
+    pl.semaphore_wait(pltpu.get_barrier_semaphore(), len(peers))
+    for copy in pair_copies:
+        copy.start()
+    forward(0, 0)
+    for load in loads[1:4]:
         load.wait()
     grad_wide = grad_ref[...].astype(F32)
-    query_flip = jnp.transpose(query_ref[...].astype(F32) * (HEAD_SIZE**-0.5))
     grad_flip = jnp.transpose(grad_wide)
     delta_flip = jnp.transpose(grad_wide * out_ref[...].astype(F32))
     aux_row = lax.broadcasted_iota(jnp.int32, (16, rows), 0)
@@ -207,7 +223,6 @@
                 rest = rest - piece
     for r in range(2):
         lanes = slice(r * half, (r + 1) * half)
-        slots[r, 0, 0:COLS, :] = query_flip[:, lanes].astype(BF16)
         slots[r, 0, COLS : 2 * COLS, :] = grad_flip[:, lanes].astype(BF16)
         slots[r, 0, 2 * COLS : 2 * COLS + 16, :] = aux[:, lanes].astype(BF16)
 
@@ -292,18 +307,14 @@
             axis=0,
         )
 
-    every = range(len(PIECES) - 1)
-
-    def forward(t, part):
-        for r in range(2):
-            slot_copy(r, t, part).start()
-
-    def pass_on(t, parts):
+    def pass_on(t, parts, always=False):
         for part in parts:
             for r in range(2):
                 slot_copy(r, t - 1, part).wait_recv()
 
             if isinstance(t, int):
+                if always:
+                    forward(t, part)
                 continue
 
             @pl.when(t < nz - 1)
@@ -311,8 +322,7 @@
                 forward(t, part)
 
     def hand_on(t, totals):
-        @pl.when(t > 1)
-        def _():
+        if not isinstance(t, int) or t > 1:
             for r in range(2):
                 trail_copy(r, t - 1).wait_recv()
 
@@ -322,8 +332,7 @@
             trail_copy(r, t).start()
 
     early = min(2, nz - 1)
-    for part in every:
-        forward(0, part)
+    forward(0, 1)
     for load in loads[4:7]:
         load.wait()
     build_keys(key_ref, value_ref, 0, seq)
@@ -348,27 +357,13 @@
         copy.wait()
     build_keys(key_other, value_other, rows, partner_seq)
 
-    def other_step(t, carry):
+    def other_step(t):
         prepare(t)
         tiles(rows)
-        totals = [early_query[r, t, :, :] + query_part(r, rows, rows) for r in range(2)]
-
-        @pl.when(t == 0)
-        def _():
-            for r in range(2):
-                early_query[r, 0, :, :] = totals[r]
-
-        @pl.when(t > 0)
-        def _():
-            hand_on(t, totals)
-
-        @pl.when(t == 0)
-        def _():
-            pass_on(t + early - 0, every)
-
-        return carry
-
-    lax.fori_loop(0, early, other_step, 0)
+        return [early_query[r, t, :, :] + query_part(r, rows, rows) for r in range(2)]
+
+    hand_on(1, other_step(1))
+    pass_on(2, every, True)
 
     def step(t, carry):
         @pl.when(t > early)
@@ -382,21 +377,31 @@
         hand_on(t, [query_part(r, 0, 2 * rows) for r in range(2)])
         return carry
 
-    lax.fori_loop(early, nz - 1, step, 0)
+    lax.fori_loop(early, early + 1, step, 0)
+    for r, total in enumerate(other_step(0)):
+        early_query[r, 0, :, :] = total
+    lax.fori_loop(early + 1, nz - 1, step, 0)
     last = nz - 1
     for load in loads[7:]:
         load.wait()
     pass_on(last, every[1:])
     prepare(last)
-    tiles(rows)
     part_copies = []
-    for m, total in enumerate((key_sum, value_sum)):
-        part_send[m, :, :] = total[rows:, :].astype(BF16)
-        copy = remote(
-            part_send.at[m], part_recv.at[m], part_sems.at[0, m], part_sems.at[1, m], partner
-        )
-        copy.start()
-        part_copies.append(copy)
+    for c in range(rows // CHUNK):
+        here = slice(c * CHUNK, (c + 1) * CHUNK)
+        for r in range(2):
+            tile(r, rows + c * CHUNK)
+        for m, total in enumerate((key_sum, value_sum)):
+            part_send[m, here, :] = total[rows + c * CHUNK : rows + (c + 1) * CHUNK, :].astype(BF16)
+            copy = remote(
+                part_send.at[m, pl.ds(c * CHUNK, CHUNK)],
+                part_recv.at[m, pl.ds(c * CHUNK, CHUNK)],
+                part_sems.at[0, m, c],
+                part_sems.at[1, m, c],
+                partner,
+            )
+            copy.start()
+            part_copies.append(copy)
     tiles(0)
     hand_on(last, [query_part(r, 0, 2 * rows) for r in range(2)])
     started = list(part_copies)
@@ -519,52 +524,93 @@
         )
 
     x_copies = {}
-
-    def x_message(r, i):
-        if i >= 2:
-            x_copies[r, i - 2].wait_recv()
-            total = x_term[r, :, :] + x_recv[r, i - 2, :, :].astype(F32)
-            x_send[r, i, :, :] = total.astype(BF16)
-        x_copies[r, i] = launch(
-            remote(
-                x_send.at[r, i], x_recv.at[r, i], x_sems.at[0, r, i], x_sems.at[1, r, i], x_ahead[r]
-            )
-        )
-
-    def input_pair(dx):
+    fourth = half // 2
+
+    def x_message(kind, r, i):
+        send, recv, sems = ((xa_send, xa_recv, xa_sems), (xb_send, xb_recv, xb_sems))[kind]
+        x_copies[kind, r, i] = launch(
+            remote(send.at[r, i], recv.at[r, i], sems.at[0, r, i], sems.at[1, r, i], x_ahead[r])
+        )
+
+    y_copies = {}
+
+    def x_pair(dx):
         total = input_term(dx, core)
         core_copies[dx].wait_recv()
         total = total + core_recv[dx, :, :].astype(F32)
-        return [total[:, y_at * COLS : (y_at + 1) * COLS] for y_at in range(2)]
-
-    def x_first():
-        sides = input_pair(2)
-        for r in range(2):
-            x_send[r, 0, :, :] = sides[r].astype(BF16)
-            x_message(r, 0)
-
-    def x_second(r):
-        sides = input_pair(1 if r == 0 else nx - 1)
-        x_send[r, 1, :, :] = sides[1 - r].astype(BF16)
-        x_message(r, 1)
-        x_term[r, :, :] = sides[r]
-
-    def x_own():
-        for y_at, total in enumerate(input_pair(0)):
-            own_term[y_at, :, :] = total
-
-    def x_final():
+        sides = [total[:, y_at * COLS : (y_at + 1) * COLS] for y_at in range(2)]
+        for r in range(2):
+            if dx == 2:
+                xa_send[r, 0, :, :] = sides[r][:half, :].astype(BF16)
+                x_message(0, r, 0)
+            elif dx == (1, nx - 1)[r]:
+                xa_send[r, 1, :, :] = sides[1 - r][:half, :].astype(BF16)
+                x_message(0, r, 1)
+                xa_term[r, :, :] = sides[r][:half, :]
+            elif dx == 0:
+                xa_own[r, :, :] = sides[r][:half, :]
+        low, high = sides[0][half:, :], sides[1][half:, :]
+        yb_send[dx, :, :] = jnp.where(low_side == 0, high, low).astype(BF16)
+        yb_term[dx, :, :] = jnp.where(low_side == 0, low, high)
+        y_copies[dx] = launch(
+            remote(
+                yb_send.at[dx], yb_recv.at[dx], y_sems.at[0, dx], y_sems.at[1, dx], neighbour
+            )
+        )
+
+    def xa_third(r):
+        x_copies[0, r, 0].wait_recv()
+        xa_send[r, 2, :, :] = (xa_term[r, :, :] + xa_recv[r, 0, :, :].astype(F32)).astype(BF16)
+        x_message(0, r, 2)
+
+    def xb_block(dx):
+        y_copies[dx].wait_recv()
+        yb_term[dx, :, :] += yb_recv[dx, :, :].astype(F32)
+
+    def xb_part(dx, part):
+        return yb_term[dx, part * fourth : (part + 1) * fourth, :]
+
+    def xb_first():
+        xb_block(2)
+        for r in range(2):
+            xb_send[r, 0, :, :] = xb_part(2, r).astype(BF16)
+            x_message(1, r, 0)
+
+    def xb_second(r):
+        dx = (1, nx - 1)[r]
+        xb_block(dx)
+        xb_send[r, 1, :, :] = xb_part(dx, 1 - r).astype(BF16)
+        x_message(1, r, 1)
+
+    def xb_third(r):
+        x_copies[1, r, 0].wait_recv()
+        total = xb_part((1, nx - 1)[r], r) + xb_recv[r, 0, :, :].astype(F32)
+        xb_send[r, 2, :, :] = total.astype(BF16)
+        x_message(1, r, 2)
+
+    def xb_final():
+        for part in range(2):
+            total = xb_part(0, part)
+            for r in range(2):
+                i = 2 if r == part else 1
+                x_copies[1, r, i].wait_recv()
+                total = total + xb_recv[r, i, :, :].astype(F32)
+            input_out[half + part * fourth : half + (part + 1) * fourth, :] = total.astype(BF16)
+
+    def xa_final():
         totals = []
         for y_at in range(2):
-            total = own_term[y_at, :, :]
+            total = xa_own[y_at, :, :]
             for r in range(2):
                 i = 2 if r == y_at else 1
-                x_copies[r, i].wait_recv()
-                total = total + x_recv[r, i, :, :].astype(F32)
+                x_copies[0, r, i].wait_recv()
+                total = total + xa_recv[r, i, :, :].astype(F32)
             totals.append(total)
-        y_send[...] = jnp.where(low_side == 0, totals[1], totals[0]).astype(BF16)
-        own_term[0, :, :] = jnp.where(low_side == 0, totals[0], totals[1])
-        return launch(remote(y_send, y_recv, y_sems.at[0], y_sems.at[1], neighbour))
+        ya_send[...] = jnp.where(low_side == 0, totals[1], totals[0]).astype(BF16)
+        xa_own[0, :, :] = jnp.where(low_side == 0, totals[0], totals[1])
+        return launch(
+            remote(ya_send, ya_recv, y_sems.at[0, nx], y_sems.at[1, nx], neighbour)
+        )
 
     def drain(t, carry):
         for r in range(2):
@@ -579,41 +625,55 @@
     for i in range(2, nz - 1):
         z_term(0, i)
     lax.fori_loop(0, nz - 1, drain, 0)
-    for m, total in ((1, key_sum), (2, value_sum)):
-        part_copies[m - 1].wait_recv()
-        low = (total[0:rows, :] + part_recv[m - 1, :, :].astype(F32)).astype(BF16)
-        grads_ref[:, m * COLS : (m + 1) * COLS] = low
-        flipped_ref[m * COLS : (m + 1) * COLS, :] = jnp.transpose(low.astype(F32)).astype(BF16)
+    for c in range(rows // CHUNK):
+        here = slice(c * CHUNK, (c + 1) * CHUNK)
+        for m, total in ((1, key_sum), (2, value_sum)):
+            part_copies[2 * c + m - 1].wait_recv()
+            low = (total[here, :] + part_recv[m - 1, here, :].astype(F32)).astype(BF16)
+            grads_ref[here, m * COLS : (m + 1) * COLS] = low
+            flipped_ref[m * COLS : (m + 1) * COLS, here] = jnp.transpose(
+                low.astype(F32)
+            ).astype(BF16)
     z_message(1, 0)
+    z_message(1, 1)
     core_message(2)
-    z_message(1, 1)
     core_message(1)
+    x_pair(2)
     z_message(0, 2, True)
     z_message(0, 3, True)
-    x_first()
     core_message(3)
-    x_second(0)
+    x_pair(1)
+    z_term(1, 2)
+    z_term(1, 3)
     core_message(0)
-    x_second(1)
-    z_message(1, 2)
-    z_message(1, 3)
+    z_message(1, 2, True)
+    z_message(1, 3, True)
+    x_pair(3)
+    x_pair(0)
     z_message(0, 4, True)
     z_message(0, 5, True)
-    x_own()
-    z_near(1)
-    for i in range(4, nz - 1):
-        z_term(1, i)
-    x_message(0, 2)
-    x_message(1, 2)
+    xb_first()
+    xa_third(0)
+    xa_third(1)
+    z_term(1, 4)
+    z_term(1, 5)
     z_message(1, 4, True)
     z_message(1, 5, True)
+    z_near(1)
+    z_term(1, 6)
+    xb_second(0)
+    xb_second(1)
     z_message(0, 6, True)
     z_message(1, 6, True)
+    xb_third(0)
+    xb_third(1)
+    xb_block(0)
+    y_copy = xa_final()
+    xb_final()
     z_final(0)
-    y_copy = x_final()
+    y_copy.wait_recv()
+    input_out[0:half, :] = (xa_own[0, :, :] + ya_recv[...].astype(F32)).astype(BF16)
     z_final(1)
-    y_copy.wait_recv()
-    input_out[...] = (own_term[0, :, :] + y_recv[...].astype(F32)).astype(BF16)
     for copy in started:
         copy.wait_send()
 
@@ -683,12 +743,17 @@
             low(wide, rows),
             low(nx, rows, 2 * COLS),
             low(nx, rows, 2 * COLS),
-            low(2, 3, rows, COLS),
-            low(2, 3, rows, COLS),
-            full(2, rows, COLS),
-            full(2, rows, COLS),
-            low(rows, COLS),
-            low(rows, COLS),
+            low(2, 3, half, COLS),
+            low(2, 3, half, COLS),
+            full(2, half, COLS),
+            full(2, half, COLS),
+            low(2, 3, half // 2, COLS),
+            low(2, 3, half // 2, COLS),
+            low(nx, half, COLS),
+            low(nx, half, COLS),
+            full(nx, half, COLS),
+            low(half, COLS),
+            low(half, COLS),
             full(2, nz - 1, COLS, COLS),
             low(2, nz - 1, COLS, COLS),
             low(2, nz - 3, COLS, COLS),
@@ -704,10 +769,11 @@
             dma((2, len(PIECES) - 1, 2, nz)),
             dma((2, 2, nz + 1)),
             dma((2, 2)),
-            dma((2, 2)),
+            dma((2, 2, rows // CHUNK)),
             dma((2, nx)),
             dma((2, 2, 3)),
-            dma((2,)),
+            dma((2, 2, 3)),
+            dma((2, nx + 1)),
             dma((2, 2, 2, nz - 1)),
             dma((2, 2, 2)),
             dma((2, 2)),

time: 78.8 us -> 76.4 us (0.970); the launches traced: 78.7 us -> 75.2 us
  Pallas kernels: 76.8 us -> 73.3 us
    pallas_call x1, Pallas kernels: 76.8 us -> 73.3 us  [local(): pl.pallas_call(functools.partial(backward_kernel, nz, nx), out_shape=(plt...]
where the time goes in v4:
time: 76.4 us; the launch traced here: 75.2 us
  Pallas kernels  73.3 us (96%)
  local copies, waits for them, and re-layouts  1.33 us (2%)
    pallas_call x1, Pallas kernels, local(): pl.pallas_call(functools.partial(backward_kernel, nz, nx), out_shape=(plt...  73.3 us

profile of v4, /device:TPU:2, one launch (start us, length us, event | category | flops | bytes accessed | tf_op | source)
XLA Modules:
  0.0 75.2 jit_solution(7786600672030191264)
XLA Ops:
  0.6 73.3 %attention_backward.1 = (bf16[512,128]{1,0:T(8,128)(2,1)S(1)}, f32[3,128,128]{2,1,0:T(8,128)S(1)}) custom-call(s32[128]{0:T(128)} %frames_hbm.1, f32[2,512]{1,0:T(2,128)} %bitcast.1, bf16[512,128]{1,0:T(8,128)(2,1)} %query_hbm.1, bf16[512,128]{1,0:T(8,128)(2,1)} %key_hbm.1, bf16[512,128]{1,0:T(8,128)(2,1)} %value_hbm.1, bf16[512,128]{1,0:T(8,128)(2,1)} %out_hbm.1, ...), custom_call_target="tpu_custom_call" | custom-call | tf_op jit(solution)/shard_map/attention_backward/pallas_call | solution.py:708
  73.9 0.7 copy.13
  74.6 0.7 copy.14

commit v5 on v4

--- a/solution.py
+++ b/solution.py
@@ -307,19 +307,18 @@
             axis=0,
         )
 
-    def pass_on(t, parts, always=False):
+    def pass_on(t, parts, onward=None):
         for part in parts:
             for r in range(2):
                 slot_copy(r, t - 1, part).wait_recv()
-
-            if isinstance(t, int):
-                if always:
-                    forward(t, part)
-                continue
-
-            @pl.when(t < nz - 1)
-            def _(part=part):
-                forward(t, part)
+                if onward is None:
+
+                    @pl.when(t < nz - 1)
+                    def _(r=r, part=part):
+                        slot_copy(r, t, part).start()
+
+                elif onward:
+                    slot_copy(r, t, part).start()
 
     def hand_on(t, totals):
         if not isinstance(t, int) or t > 1:
@@ -384,7 +383,7 @@
     last = nz - 1
     for load in loads[7:]:
         load.wait()
-    pass_on(last, every[1:])
+    pass_on(last, every[1:], False)
     prepare(last)
     part_copies = []
     for c in range(rows // CHUNK):
@@ -634,45 +633,45 @@
             flipped_ref[m * COLS : (m + 1) * COLS, here] = jnp.transpose(
                 low.astype(F32)
             ).astype(BF16)
+    core_message(2)
+    core_message(3)
     z_message(1, 0)
+    core_message(1)
     z_message(1, 1)
-    core_message(2)
-    core_message(1)
     x_pair(2)
+    core_message(0)
+    z_term(1, 2)
     z_message(0, 2, True)
+    x_pair(3)
+    z_near(1)
+    z_message(1, 2, True)
+    x_pair(1)
+    z_term(1, 4)
     z_message(0, 3, True)
-    core_message(3)
-    x_pair(1)
-    z_term(1, 2)
+    z_term(1, 6)
     z_term(1, 3)
-    core_message(0)
-    z_message(1, 2, True)
+    xa_third(0)
+    xa_third(1)
+    z_term(1, 5)
+    xb_first()
     z_message(1, 3, True)
-    x_pair(3)
+    xb_second(1)
     x_pair(0)
     z_message(0, 4, True)
     z_message(0, 5, True)
-    xb_first()
-    xa_third(0)
-    xa_third(1)
-    z_term(1, 4)
-    z_term(1, 5)
     z_message(1, 4, True)
+    y_copy = xa_final()
+    xb_second(0)
     z_message(1, 5, True)
-    z_near(1)
-    z_term(1, 6)
-    xb_second(0)
-    xb_second(1)
     z_message(0, 6, True)
-    z_message(1, 6, True)
+    xb_block(0)
     xb_third(0)
     xb_third(1)
-    xb_block(0)
-    y_copy = xa_final()
-    xb_final()
-    z_final(0)
+    z_message(1, 6, True)
     y_copy.wait_recv()
     input_out[0:half, :] = (xa_own[0, :, :] + ya_recv[...].astype(F32)).astype(BF16)
+    z_final(0)
+    xb_final()
     z_final(1)
     for copy in started:
         copy.wait_send()

time: 76.4 us -> 75.9 us (level); the launches traced: 75.2 us -> 75.8 us
  no operation moved by 1% of the time
where the time goes in v5:
time: 75.9 us; the launch traced here: 75.8 us
  Pallas kernels  73.9 us (97%)
  local copies, waits for them, and re-layouts  1.33 us (2%)
    pallas_call x1, Pallas kernels, local(): pl.pallas_call(functools.partial(backward_kernel, nz, nx), out_shape=(plt...  73.9 us

profile of v5, /device:TPU:2, one launch (start us, length us, event | category | flops | bytes accessed | tf_op | source)
XLA Modules:
  0.0 75.8 jit_solution(6897184886546908093)
XLA Ops:
  0.6 73.9 %attention_backward.1 = (bf16[512,128]{1,0:T(8,128)(2,1)S(1)}, f32[3,128,128]{2,1,0:T(8,128)S(1)}) custom-call(s32[128]{0:T(128)} %frames_hbm.1, f32[2,512]{1,0:T(2,128)} %bitcast.1, bf16[512,128]{1,0:T(8,128)(2,1)} %query_hbm.1, bf16[512,128]{1,0:T(8,128)(2,1)} %key_hbm.1, bf16[512,128]{1,0:T(8,128)(2,1)} %value_hbm.1, bf16[512,128]{1,0:T(8,128)(2,1)} %out_hbm.1, ...), custom_call_target="tpu_custom_call" | custom-call | tf_op jit(solution)/shard_map/attention_backward/pallas_call | solution.py:707
  74.5 0.7 copy.13
  75.2 0.7 copy.14

commit v6 on v5

--- a/solution.py
+++ b/solution.py
@@ -123,25 +123,6 @@
     last_sems,
     near_sems,
 ):
-    loads = [
-        pltpu.make_async_copy(source, target, load_sems.at[i])
-        for i, (source, target) in enumerate(
-            (
-                (query_hbm, query_ref),
-                (grad_hbm, grad_ref),
-                (out_hbm, out_ref),
-                (stat_hbm, stat_ref),
-                (key_hbm, key_ref),
-                (value_hbm, value_ref),
-                (frames_hbm, frames_ref),
-                (input_hbm, input_ref),
-                (weight_hbm, weight_ref),
-            )
-        )
-    ]
-    for load in loads:
-        load.start()
-
     rows = query_ref.shape[0]
     half = rows // 2
     blocks = rows // BLOCK
@@ -166,6 +147,25 @@
     slants = [{"seq": 2 * lax.rem(z + dz, nz) + 1 - side} for dz in (1, nz - 1)]
     peers = (*z_ahead, partner, *slants, twin, neighbour, *x_ahead)
     greet(peers)
+    loads = [
+        pltpu.make_async_copy(source, target, load_sems.at[i])
+        for i, (source, target) in enumerate(
+            (
+                (query_hbm, query_ref),
+                (grad_hbm, grad_ref),
+                (out_hbm, out_ref),
+                (stat_hbm, stat_ref),
+                (key_hbm, key_ref),
+                (value_hbm, value_ref),
+                (frames_hbm, frames_ref),
+                (input_hbm, input_ref),
+                (weight_hbm, weight_ref),
+            )
+        )
+    ]
+    for load in loads[:7]:
+        load.start()
+
 
     pair_copies = [
         remote(key_hbm, key_other, pair_sems.at[0, 0], pair_sems.at[1, 0], partner),
@@ -332,6 +332,8 @@
 
     early = min(2, nz - 1)
     forward(0, 1)
+    for load in loads[7:]:
+        load.start()
     for load in loads[4:7]:
         load.wait()
     build_keys(key_ref, value_ref, 0, seq)
@@ -620,10 +622,6 @@
 
     z_message(0, 0)
     z_message(0, 1)
-    z_near(0)
-    for i in range(2, nz - 1):
-        z_term(0, i)
-    lax.fori_loop(0, nz - 1, drain, 0)
     for c in range(rows // CHUNK):
         here = slice(c * CHUNK, (c + 1) * CHUNK)
         for m, total in ((1, key_sum), (2, value_sum)):
@@ -641,13 +639,14 @@
     x_pair(2)
     core_message(0)
     z_term(1, 2)
-    z_message(0, 2, True)
+    z_message(0, 2)
     x_pair(3)
     z_near(1)
+    z_near(0)
     z_message(1, 2, True)
     x_pair(1)
     z_term(1, 4)
-    z_message(0, 3, True)
+    z_message(0, 3)
     z_term(1, 6)
     z_term(1, 3)
     xa_third(0)
@@ -657,13 +656,13 @@
     z_message(1, 3, True)
     xb_second(1)
     x_pair(0)
-    z_message(0, 4, True)
-    z_message(0, 5, True)
+    z_message(0, 4)
+    z_message(0, 5)
     z_message(1, 4, True)
     y_copy = xa_final()
     xb_second(0)
     z_message(1, 5, True)
-    z_message(0, 6, True)
+    z_message(0, 6)
     xb_block(0)
     xb_third(0)
     xb_third(1)
@@ -673,6 +672,7 @@
     z_final(0)
     xb_final()
     z_final(1)
+    lax.fori_loop(0, nz - 1, drain, 0)
     for copy in started:
         copy.wait_send()
 

time: 75.9 us -> 76.3 us (level)
  no operation moved by 1% of the time
where the time goes in v6:
time: 76.3 us; the launch traced here: 76.2 us
  Pallas kernels  74.2 us (97%)
  local copies, waits for them, and re-layouts  1.33 us (2%)
    pallas_call x1, Pallas kernels, local(): pl.pallas_call(functools.partial(backward_kernel, nz, nx), out_shape=(plt...  74.2 us

profile of v6, /device:TPU:2, one launch (start us, length us, event | category | flops | bytes accessed | tf_op | source)
XLA Modules:
  0.0 76.2 jit_solution(3059106229981596336)
XLA Ops:
  0.6 74.2 %attention_backward.1 = (bf16[512,128]{1,0:T(8,128)(2,1)S(1)}, f32[3,128,128]{2,1,0:T(8,128)S(1)}) custom-call(s32[128]{0:T(128)} %frames_hbm.1, f32[2,512]{1,0:T(2,128)} %bitcast.1, bf16[512,128]{1,0:T(8,128)(2,1)} %query_hbm.1, bf16[512,128]{1,0:T(8,128)(2,1)} %key_hbm.1, bf16[512,128]{1,0:T(8,128)(2,1)} %value_hbm.1, bf16[512,128]{1,0:T(8,128)(2,1)} %out_hbm.1, ...), custom_call_target="tpu_custom_call" | custom-call | tf_op jit(solution)/shard_map/attention_backward/pallas_call | solution.py:707
  74.9 0.7 copy.13
  75.5 0.7 copy.14
